TPU v7x, 128 devices: a whole 4x4x4 slice. The times are simulated.
128 devices in a mesh: grid: 32 (over x_lo, z, y), mem: 4 (over x_hi, core).
Axes of the slice: x: 4 (x_hi: 2, x_lo: 2; x = x_hi * 2 + x_lo), y: 4, z: 4, core: 2. Of those that a mesh axis runs over, the one named last changes fastest.
Arguments:
- field: bfloat16 [512, 2, 512, 1024], P('mem', None, 'grid'), may hold values from -6 to 6
- winds: bfloat16 [2, 2, 512, 1024], P(None, None, 'grid'), may hold values from -0.44921875 to 0.44921875
- obs_index: int32 [512, 3072], P('grid'), may hold values from 0 to 524287, as said below
- measured_values: float32 [512, 3072], P('grid'), may hold values from -6 to 6
- precision_weights: float32 [512, 3072], P('grid'), may hold values from 0.05 to 1
Outputs:
- gram: float32 [512, 512, 512], P('grid', 'mem')
- proj: float32 [512, 512], P('grid', 'mem')
Inputs may be any that keep to these rules, and one draw needn't show every extreme that they name: obs_index holds row * 1024 + column; an observation of patch p lies in rows (p // 16) * 16 - 8 to (p // 16 + 1) * 16 + 7 and columns (p % 16) * 64 - 8 to (p % 16 + 1) * 64 + 7, clipped to the grid; cells may repeat.
All inputs are finite; a program needn't handle non-finite values.
Results may differ from a plain program's by a relative error of at most 0.005.
Values may be sent and summed in bfloat16 or wider, within the bound.
No kernel may reach another device: no remote copies, remote signals or barrier semaphores. Data moves between devices by JAX's collectives and lax.ppermute only.
A program may use at most 320 MiB of HBM per device.

v0:
```python
import jax
import jax.numpy as jnp
from jax import lax
from jax.sharding import PartitionSpec as P

PATCH_C = 64
HALO_R = 8


LOC_AREA = 512.0
LOW_SHARE = 0.7
HIGH_SHARE = 0.3


def with_halo(block, sides, width):
    for axis, dim in sides:
        count = lax.axis_size(axis)
        forward = [(i, i + 1) for i in range(count - 1)]
        backward = [(target, source) for source, target in forward]
        low = lax.ppermute(
            lax.slice_in_dim(block, block.shape[dim] - width, None, axis=dim), axis, forward
        )
        high = lax.ppermute(lax.slice_in_dim(block, 0, width, axis=dim), axis, backward)
        block = jnp.concatenate([low, block, high], axis=dim)
    return block


def advect_rows(extended, flow_rows, flow_cols):
    middle = extended[..., 1:-1, :]
    above = extended[..., :-2, :]
    below = extended[..., 2:, :]
    widths = [(0, 0)] * (middle.ndim - 1) + [(1, 1)]
    padded = jnp.pad(middle, widths)
    left = padded[..., :-2]
    right = padded[..., 2:]
    return (
        middle
        - jnp.maximum(flow_rows, 0.0) * (middle - above)
        - jnp.minimum(flow_rows, 0.0) * (below - middle)
        - jnp.maximum(flow_cols, 0.0) * (middle - left)
        - jnp.minimum(flow_cols, 0.0) * (right - middle)
    )


def column_mix(state):
    mixed = LOW_SHARE * state[:, 0] + HIGH_SHARE * state[:, 1]
    return jnp.moveaxis(mixed, 0, -1).astype(jnp.bfloat16)


def per_device(field, winds, obs_index, measured_values, precision_weights):
    mine = field.shape[0]
    rows = field.shape[2]
    width = field.shape[3]
    members = mine * lax.axis_size("mem")
    row_start = lax.axis_index("grid") * rows
    patch_count = obs_index.shape[0]
    centre_row = row_start.astype(jnp.float32) + (rows - 1) * 0.5
    centre_col = (jnp.arange(patch_count, dtype=jnp.int32) * PATCH_C).astype(jnp.float32)[
        :, None
    ] + (PATCH_C - 1) * 0.5
    row_diff = (obs_index // width).astype(jnp.float32) - centre_row
    col_diff = (obs_index % width).astype(jnp.float32) - centre_col
    distance = row_diff * row_diff + col_diff * col_diff
    weight = precision_weights * jnp.exp(-distance / LOC_AREA)
    root = jnp.sqrt(weight / (members - 1.0))
    nearby_index = (obs_index // width - row_start + HALO_R) * width + obs_index % width
    state = field.astype(jnp.float32)
    flows = winds.astype(jnp.float32)
    for step in range(2):
        extended = with_halo(state, (("grid", 2),), 1)
        state = advect_rows(extended, flows[0], flows[1])
    cellwise = column_mix(state)
    everyone = lax.all_gather(cellwise, "mem", axis=2, tiled=True)
    widened = with_halo(everyone, (("grid", 0),), HALO_R)
    flat = widened.reshape(-1, members)
    own_start = lax.axis_index("mem") * mine

    def one_patch(items):
        index, root_patch, values = items
        seen = jnp.take(flat, index, axis=0)
        mean = jnp.sum(seen.astype(jnp.float32), axis=1) / members
        scaled = (root_patch[:, None] * (seen.astype(jnp.float32) - mean[:, None])).astype(
            jnp.bfloat16
        )
        innov = (root_patch * (values - mean)).astype(jnp.bfloat16)
        own = lax.dynamic_slice_in_dim(scaled, own_start, mine, 1)
        gram_patch = jnp.einsum("km,kn->mn", own, scaled, preferred_element_type=jnp.float32)
        proj_patch = jnp.einsum("km,k->m", own, innov, preferred_element_type=jnp.float32)
        return (gram_patch, proj_patch)

    gram, proj = lax.map(one_patch, (nearby_index, root, measured_values))
    return (gram, proj)


def solution(mesh):
    return jax.shard_map(
        per_device,
        mesh=mesh,
        in_specs=(
            P("mem", None, "grid", None),
            P(None, None, "grid", None),
            P("grid", None),
            P("grid", None),
            P("grid", None),
        ),
        out_specs=(P("grid", "mem", None), P("grid", "mem")),
        check_vma=False,
    )
```

profile of v0, /device:TPU:3, one launch (start us, length us, event | category | flops | bytes accessed | tf_op | source)
XLA Modules:
  0.0 1258.8 jit_solution(8285986978272887992)
XLA Ops:
  7.2 14.0 %copy_convert_fusion = f32[128,2,16,1024]{3,0,2,1:T(8,128)} fusion(bf16[128,2,16,1024]{3,2,1,0:T(8,128)(2,1)} %param.7), kind=kLoop, calls=%fused_computation.59 | loop fusion | flops 4194304 | bytes 25165824 | tf_op jit(solution)/shard_map/convert_element_type | solution.py:67
  22.9 3.2 collective-permute-start
  26.1 6.8 collective-permute-start.1
  33.0 20.8 %collective-permute-done = f32[128,2,1,1024]{3,0,2,1:T(8,128)S(1)} collective-permute-done((f32[128,2,1,1024]{3,0,2,1:T(8,128)S(1)}, f32[128,2,1,1024]{3,0,2,1:T(8,128)S(1)}, u32[]{:S(2)}, u32[]{:S(2)}) %collective-permute-start) | collective-permute-done | bytes 1048608 | tf_op jit(solution)/shard_map/ppermute | solution.py:20
  54.7 31.8 %fusion.17 = f32[128,2,16,1024]{3,0,2,1:T(8,128)} fusion(f32[128,2,16,1024]{3,0,2,1:T(8,128)} %copy_convert_fusion, f32[128,2,1,1024]{3,0,2,1:T(8,128)S(1)} %collective-permute-done.1, f32[128,2,1,1024]{3,0,2,1:T(8,128)S(1)} %collective-permute-done, f32[2,16,1024]{2,1,0:T(8,128)S(1)} %get-tuple-element.139, f32[2,16,1024]{2,1,0:T(8,128)S(1)} %get-tuple-element.140, ...), kind=kLoop, calls=%fused_computation.41 | loop fusion | flops 62914560 | bytes 44564480 | tf_op jit(solution)/shard_map/sub | solution.py:37
  90.1 8.5 collective-permute-start.3
  98.7 19.8 %collective-permute-done.2 = f32[128,2,1,1024]{3,0,2,1:T(8,128)S(1)} collective-permute-done((f32[128,2,1,1024]{3,0,2,1:T(8,128)S(1)}, f32[128,2,1,1024]{3,0,2,1:T(8,128)S(1)}, u32[]{:S(2)}, u32[]{:S(2)}) %collective-permute-start.2) | collective-permute-done | bytes 1048608 | tf_op jit(solution)/shard_map/ppermute | solution.py:20
  119.4 33.8 %fusion.11 = f32[128,2,16,1024]{3,0,2,1:T(8,128)} fusion(f32[128,2,16,1024]{3,0,2,1:T(8,128)} %fusion.17, f32[128,2,1,1024]{3,0,2,1:T(8,128)S(1)} %collective-permute-done.3, f32[128,2,1,1024]{3,0,2,1:T(8,128)S(1)} %collective-permute-done.2, f32[2,16,1024]{2,1,0:T(8,128)S(1)} %get-tuple-element.139, f32[2,16,1024]{2,1,0:T(8,128)S(1)} %get-tuple-element.140, ...), kind=kLoop, calls=%fused_computation.35 | loop fusion | flops 58720256 | bytes 36175872 | tf_op jit(solution)/shard_map/sub | solution.py:37
  153.2 7.1 fusion.29
  160.3 4.3 copy.10
  164.6 113.8 %all-gather.2.cloned.1.call-done = bf16[16,1024,512]{1,0,2:T(8,128)(2,1)} async-done(((bf16[16,1024,128]{1,0,2:T(8,128)(2,1)}), bf16[16,1024,512]{1,0,2:T(8,128)(2,1)}) %all-gather.2.cloned.1.call-update) | async-done | bytes 16777232 | tf_op jit(solution)/shard_map/all_gather | solution.py:73
  278.5 11.6 fusion.32
  290.1 3.1 collective-permute-start.4
  293.2 6.5 collective-permute-start.5
  300.9 177.5 %collective-permute-done.4 = bf16[8,1024,512]{1,0,2:T(8,128)(2,1)} collective-permute-done((bf16[8,1024,512]{1,0,2:T(8,128)(2,1)}, bf16[8,1024,512]{1,0,2:T(8,128)(2,1)}, u32[]{:S(2)}, u32[]{:S(2)}) %collective-permute-start.4) | collective-permute-done | bytes 8388640 | tf_op jit(solution)/shard_map/ppermute | solution.py:20
  479.3 22.7 %pad_maximum_fusion = bf16[32,1024,512]{1,0,2:T(8,128)(2,1)} fusion(bf16[8,1024,512]{1,0,2:T(8,128)(2,1)} %collective-permute-done.5, bf16[16,1024,512]{1,0,2:T(8,128)(2,1)} %all-gather.2.cloned.1.call-done, bf16[8,1024,512]{1,0,2:T(8,128)(2,1)} %collective-permute-done.4), kind=kLoop, calls=%fused_computation.22 | loop fusion | flops 100663296 | bytes 67108864 | tf_op jit(solution)/shard_map/concatenate | solution.py:24
  502.0 45.5 %copy.12 = bf16[32,1024,512]{2,1,0:T(8,128)(2,1)} copy(bf16[32,1024,512]{1,0,2:T(8,128)(2,1)} %pad_maximum_fusion) | data formatting | bytes 67108864 | tf_op jit(solution)/shard_map/while | solution.py:91
  547.5 704.5 %while.14 = (s32[]{:T(128)}, f32[16,128,512]{2,1,0:T(8,128)}, f32[16,128]{1,0:T(8,128)}, f32[16,3072]{1,0:T(8,128)}, s32[16,3072]{1,0:T(8,128)S(1)}, /*index=5*/...) while((s32[]{:T(128)}, f32[16,128,512]{2,1,0:T(8,128)}, ...), condition=%wide.region_2.3_spmd, body=%wide.region_0.2_spmd.sunk | while | flops 416062464 | bytes 20973172 | solution.py:91
  547.5 35.3 %gather_fusion = bf16[3072,512]{1,0:T(8,128)(2,1)S(1)} fusion(bf16[32768,512]{1,0:T(8,128)(2,1)} %get-tuple-element.227, s32[3072]{0:T(1024)S(1)} %broadcast_clamp_fusion.2), kind=kCustom, calls=%fused_computation.clone.1 | custom fusion | bytes 6303744 | tf_op jit(solution)/shard_map/while/body/eval_jaxpr/jit(_take)/gather | solution.py:80
  582.8 2.1 convert_reduce_fusion.2
  585.9 2.7 fusion.48
  591.6 35.3 %gather_fusion = bf16[3072,512]{1,0:T(8,128)(2,1)S(1)} fusion(bf16[32768,512]{1,0:T(8,128)(2,1)} %get-tuple-element.227, s32[3072]{0:T(1024)S(1)} %broadcast_clamp_fusion.2), kind=kCustom, calls=%fused_computation.clone.1 | custom fusion | bytes 6303744 | tf_op jit(solution)/shard_map/while/body/eval_jaxpr/jit(_take)/gather | solution.py:80
  626.8 2.1 convert_reduce_fusion.2
  630.0 2.7 fusion.48
  635.6 35.3 %gather_fusion = bf16[3072,512]{1,0:T(8,128)(2,1)S(1)} fusion(bf16[32768,512]{1,0:T(8,128)(2,1)} %get-tuple-element.227, s32[3072]{0:T(1024)S(1)} %broadcast_clamp_fusion.2), kind=kCustom, calls=%fused_computation.clone.1 | custom fusion | bytes 6303744 | tf_op jit(solution)/shard_map/while/body/eval_jaxpr/jit(_take)/gather | solution.py:80
  670.9 2.1 convert_reduce_fusion.2
  674.0 2.7 fusion.48
  679.6 35.3 %gather_fusion = bf16[3072,512]{1,0:T(8,128)(2,1)S(1)} fusion(bf16[32768,512]{1,0:T(8,128)(2,1)} %get-tuple-element.227, s32[3072]{0:T(1024)S(1)} %broadcast_clamp_fusion.2), kind=kCustom, calls=%fused_computation.clone.1 | custom fusion | bytes 6303744 | tf_op jit(solution)/shard_map/while/body/eval_jaxpr/jit(_take)/gather | solution.py:80
  714.9 2.1 convert_reduce_fusion.2
  718.0 2.7 fusion.48
  723.6 35.3 %gather_fusion = bf16[3072,512]{1,0:T(8,128)(2,1)S(1)} fusion(bf16[32768,512]{1,0:T(8,128)(2,1)} %get-tuple-element.227, s32[3072]{0:T(1024)S(1)} %broadcast_clamp_fusion.2), kind=kCustom, calls=%fused_computation.clone.1 | custom fusion | bytes 6303744 | tf_op jit(solution)/shard_map/while/body/eval_jaxpr/jit(_take)/gather | solution.py:80
  758.9 2.1 convert_reduce_fusion.2
  762.0 2.7 fusion.48
  767.6 35.3 %gather_fusion = bf16[3072,512]{1,0:T(8,128)(2,1)S(1)} fusion(bf16[32768,512]{1,0:T(8,128)(2,1)} %get-tuple-element.227, s32[3072]{0:T(1024)S(1)} %broadcast_clamp_fusion.2), kind=kCustom, calls=%fused_computation.clone.1 | custom fusion | bytes 6303744 | tf_op jit(solution)/shard_map/while/body/eval_jaxpr/jit(_take)/gather | solution.py:80
  802.9 2.1 convert_reduce_fusion.2
  806.1 2.7 fusion.48
  811.7 35.3 %gather_fusion = bf16[3072,512]{1,0:T(8,128)(2,1)S(1)} fusion(bf16[32768,512]{1,0:T(8,128)(2,1)} %get-tuple-element.227, s32[3072]{0:T(1024)S(1)} %broadcast_clamp_fusion.2), kind=kCustom, calls=%fused_computation.clone.1 | custom fusion | bytes 6303744 | tf_op jit(solution)/shard_map/while/body/eval_jaxpr/jit(_take)/gather | solution.py:80
  847.0 2.1 convert_reduce_fusion.2
  850.1 2.7 fusion.48
  855.7 35.2 %gather_fusion = bf16[3072,512]{1,0:T(8,128)(2,1)S(1)} fusion(bf16[32768,512]{1,0:T(8,128)(2,1)} %get-tuple-element.227, s32[3072]{0:T(1024)S(1)} %broadcast_clamp_fusion.2), kind=kCustom, calls=%fused_computation.clone.1 | custom fusion | bytes 6303744 | tf_op jit(solution)/shard_map/while/body/eval_jaxpr/jit(_take)/gather | solution.py:80
  891.0 2.1 convert_reduce_fusion.2
  894.1 2.7 fusion.48
  899.7 35.3 %gather_fusion = bf16[3072,512]{1,0:T(8,128)(2,1)S(1)} fusion(bf16[32768,512]{1,0:T(8,128)(2,1)} %get-tuple-element.227, s32[3072]{0:T(1024)S(1)} %broadcast_clamp_fusion.2), kind=kCustom, calls=%fused_computation.clone.1 | custom fusion | bytes 6303744 | tf_op jit(solution)/shard_map/while/body/eval_jaxpr/jit(_take)/gather | solution.py:80
  935.0 2.1 convert_reduce_fusion.2
  938.1 2.7 fusion.48
  943.8 35.3 %gather_fusion = bf16[3072,512]{1,0:T(8,128)(2,1)S(1)} fusion(bf16[32768,512]{1,0:T(8,128)(2,1)} %get-tuple-element.227, s32[3072]{0:T(1024)S(1)} %broadcast_clamp_fusion.2), kind=kCustom, calls=%fused_computation.clone.1 | custom fusion | bytes 6303744 | tf_op jit(solution)/shard_map/while/body/eval_jaxpr/jit(_take)/gather | solution.py:80
  979.1 2.1 convert_reduce_fusion.2
  982.2 2.7 fusion.48
  987.8 35.3 %gather_fusion = bf16[3072,512]{1,0:T(8,128)(2,1)S(1)} fusion(bf16[32768,512]{1,0:T(8,128)(2,1)} %get-tuple-element.227, s32[3072]{0:T(1024)S(1)} %broadcast_clamp_fusion.2), kind=kCustom, calls=%fused_computation.clone.1 | custom fusion | bytes 6303744 | tf_op jit(solution)/shard_map/while/body/eval_jaxpr/jit(_take)/gather | solution.py:80
  1023.1 2.1 convert_reduce_fusion.2
  1026.2 2.7 fusion.48
  1031.9 35.3 %gather_fusion = bf16[3072,512]{1,0:T(8,128)(2,1)S(1)} fusion(bf16[32768,512]{1,0:T(8,128)(2,1)} %get-tuple-element.227, s32[3072]{0:T(1024)S(1)} %broadcast_clamp_fusion.2), kind=kCustom, calls=%fused_computation.clone.1 | custom fusion | bytes 6303744 | tf_op jit(solution)/shard_map/while/body/eval_jaxpr/jit(_take)/gather | solution.py:80
  1067.2 2.1 convert_reduce_fusion.2
  1070.3 2.7 fusion.48
  1075.9 35.3 %gather_fusion = bf16[3072,512]{1,0:T(8,128)(2,1)S(1)} fusion(bf16[32768,512]{1,0:T(8,128)(2,1)} %get-tuple-element.227, s32[3072]{0:T(1024)S(1)} %broadcast_clamp_fusion.2), kind=kCustom, calls=%fused_computation.clone.1 | custom fusion | bytes 6303744 | tf_op jit(solution)/shard_map/while/body/eval_jaxpr/jit(_take)/gather | solution.py:80
  1111.2 2.1 convert_reduce_fusion.2
  1114.3 2.7 fusion.48
  1119.9 35.2 %gather_fusion = bf16[3072,512]{1,0:T(8,128)(2,1)S(1)} fusion(bf16[32768,512]{1,0:T(8,128)(2,1)} %get-tuple-element.227, s32[3072]{0:T(1024)S(1)} %broadcast_clamp_fusion.2), kind=kCustom, calls=%fused_computation.clone.1 | custom fusion | bytes 6303744 | tf_op jit(solution)/shard_map/while/body/eval_jaxpr/jit(_take)/gather | solution.py:80
  1155.2 2.1 convert_reduce_fusion.2
  1158.3 2.7 fusion.48
  1163.9 35.3 %gather_fusion = bf16[3072,512]{1,0:T(8,128)(2,1)S(1)} fusion(bf16[32768,512]{1,0:T(8,128)(2,1)} %get-tuple-element.227, s32[3072]{0:T(1024)S(1)} %broadcast_clamp_fusion.2), kind=kCustom, calls=%fused_computation.clone.1 | custom fusion | bytes 6303744 | tf_op jit(solution)/shard_map/while/body/eval_jaxpr/jit(_take)/gather | solution.py:80
  1202.4 2.7 fusion.48
  1208.0 35.3 %gather_fusion = bf16[3072,512]{1,0:T(8,128)(2,1)S(1)} fusion(bf16[32768,512]{1,0:T(8,128)(2,1)} %get-tuple-element.227, s32[3072]{0:T(1024)S(1)} %broadcast_clamp_fusion.2), kind=kCustom, calls=%fused_computation.clone.1 | custom fusion | bytes 6303744 | tf_op jit(solution)/shard_map/while/body/eval_jaxpr/jit(_take)/gather | solution.py:80
  1246.4 2.7 fusion.48
  (167 shorter events, 75.6 us)
Async XLA Ops:
  7.2 25.8 %copy-start.2 = (bf16[2,2,16,1024]{3,2,1,0:T(8,128)(2,1)S(1)}, bf16[2,2,16,1024]{3,2,1,0:T(8,128)(2,1)}, u32[]{:S(2)}) copy-start(bf16[2,2,16,1024]{3,2,1,0:T(8,128)(2,1)} %param.8) | copy-start | bytes 393220
  7.2 271.3 %all-gather.2.cloned.1.call-start = ((), (), s32[]{:S(2)}) async-start(), calls=%async_computation | async-start | bytes 20971520 | tf_op jit(solution)/shard_map/all_gather | solution.py:73
  22.9 31.0 %collective-permute-start = (f32[128,2,1,1024]{3,0,2,1:T(8,128)S(1)}, f32[128,2,1,1024]{3,0,2,1:T(8,128)S(1)}, u32[]{:S(2)}, u32[]{:S(2)}) collective-permute-start(f32[128,2,1,1024]{3,0,2,1:T(8,128)S(1)} %get-tuple-element.135), channel_id=1, source_target_pairs={{0,4},{4,8},{8,12},{12,16},{16,20},{20,24},{24,28},{28,32},{32,36}... | collective-permute-start | bytes 3145736 | tf_op jit(solution)/shard_map/ppermute | solution.py:20
  26.1 28.6 %collective-permute-start.1 = (f32[128,2,1,1024]{3,0,2,1:T(8,128)S(1)}, f32[128,2,1,1024]{3,0,2,1:T(8,128)S(1)}, u32[]{:S(2)}, u32[]{:S(2)}) collective-permute-start(f32[128,2,1,1024]{3,0,2,1:T(8,128)S(1)} %get-tuple-element.136), channel_id=1, source_target_pairs={{4,0},{8,4},{12,8},{16,12},{20,16},{24,20},{28,24},{32,28},{36,32}... | collective-permute-start | bytes 3145736 | tf_op jit(solution)/shard_map/ppermute | solution.py:23
  88.2 30.2 %collective-permute-start.2 = (f32[128,2,1,1024]{3,0,2,1:T(8,128)S(1)}, f32[128,2,1,1024]{3,0,2,1:T(8,128)S(1)}, u32[]{:S(2)}, u32[]{:S(2)}) collective-permute-start(f32[128,2,1,1024]{3,0,2,1:T(8,128)S(1)} %get-tuple-element.133), channel_id=1, source_target_pairs={{0,4},{4,8},{8,12},{12,16},{16,20},{20,24},{24,28},{28,32},{32,36}... | collective-permute-start | bytes 3145736 | tf_op jit(solution)/shard_map/ppermute | solution.py:20
  90.1 29.2 %collective-permute-start.3 = (f32[128,2,1,1024]{3,0,2,1:T(8,128)S(1)}, f32[128,2,1,1024]{3,0,2,1:T(8,128)S(1)}, u32[]{:S(2)}, u32[]{:S(2)}) collective-permute-start(f32[128,2,1,1024]{3,0,2,1:T(8,128)S(1)} %get-tuple-element.134), channel_id=1, source_target_pairs={{4,0},{8,4},{12,8},{16,12},{20,16},{24,20},{28,24},{32,28},{36,32}... | collective-permute-start | bytes 3145736 | tf_op jit(solution)/shard_map/ppermute | solution.py:23
  164.6 135.1 %copy-start = (s32[16,3072]{1,0:T(8,128)S(1)}, s32[16,3072]{1,0:T(8,128)}, u32[]{:S(2)}) copy-start(s32[16,3072]{1,0:T(8,128)} %param.9) | copy-start | bytes 589828
  164.6 135.3 %copy-start.1 = (f32[16,3072]{1,0:T(8,128)S(1)}, f32[16,3072]{1,0:T(8,128)}, u32[]{:S(2)}) copy-start(f32[16,3072]{1,0:T(8,128)} %param.11) | copy-start | bytes 589828
  290.1 188.4 %collective-permute-start.4 = (bf16[8,1024,512]{1,0,2:T(8,128)(2,1)}, bf16[8,1024,512]{1,0,2:T(8,128)(2,1)}, u32[]{:S(2)}, u32[]{:S(2)}) collective-permute-start(bf16[8,1024,512]{1,0,2:T(8,128)(2,1)} %get-tuple-element.131), channel_id=1, source_target_pairs={{0,4},{4,8},{8,12},{12,16},{16,20},{20,24},{24,28},{28,32},{32,36}... | collective-permute-start | bytes 25165832 | tf_op jit(solution)/shard_map/ppermute | solution.py:20
  293.2 186.1 %collective-permute-start.5 = (bf16[8,1024,512]{1,0,2:T(8,128)(2,1)}, bf16[8,1024,512]{1,0,2:T(8,128)(2,1)}, u32[]{:S(2)}, u32[]{:S(2)}) collective-permute-start(bf16[8,1024,512]{1,0,2:T(8,128)(2,1)} %get-tuple-element.132), channel_id=1, source_target_pairs={{4,0},{8,4},{12,8},{16,12},{20,16},{24,20},{28,24},{32,28},{36,32}... | collective-permute-start | bytes 25165832 | tf_op jit(solution)/shard_map/ppermute | solution.py:23
Sparse Core Ops, SparseCore 0:
  164.7 113.6 all-gather.1
where the time goes:
time: 1270 us; the launch traced here: 1260 us
  local copies, waits for them, and re-layouts  666 us (52%)
  waiting for transfers between devices  335 us (26%)
  other arithmetic  189 us (15%)
  starting transfers between devices  30 us (2%)
  matrix products  25 us (2%)
  between operations  14.2 us (1%)
    gather x16, local copies, waits for them, and re-layouts, one_patch(): seen = jnp.take(flat, index, axis=0)  564 us
    ppermute x3, waiting for transfers between devices, with_halo(): lax.ppermute(lax.slice_in_dim(block, block.shape[dim] - width, None, axis...  218 us
    all_gather x1, waiting for transfers between devices, per_device(): everyone = lax.all_gather(cellwise, 'mem', axis=2, tiled=True)  114 us
    sub x2, other arithmetic, advect_rows(): middle - jnp.maximum(flow_rows, 0.0) * (middle - above)  65.6 us
    while x1, local copies, waits for them, and re-layouts, per_device(): gram, proj = lax.map(one_patch, (nearby_index, root, measured_values))  45.5 us
    convert_element_type x16, other arithmetic, one_patch(): (root_patch[:, None] * (seen.astype(jnp.float32) - mean[:, None])).astype...  43 us
    reduce_sum x16, other arithmetic, one_patch(): mean = jnp.sum(seen.astype(jnp.float32), axis=1) / members  34.2 us
  transfers between devices with their start and end apart: 7, of which 7 were waited for; matrix products, arithmetic and copies ran while one was open for 0% of the time, Pallas kernels for 0%

commit v1 on v0

v1 whole, which is shorter than its diff:
```python
import functools

import jax
import jax.numpy as jnp
from jax import lax
from jax.experimental import pallas as pl
from jax.experimental.pallas import tpu as pltpu
from jax.sharding import PartitionSpec as P

PATCH_C = 64
HALO_R = 8
LOC_AREA = 512.0
LOW_SHARE = 0.7
HIGH_SHARE = 0.3

ROWS = 16
WIDTH = 1024
MINE = 128
GROUPS = 4
MEMBERS = MINE * GROUPS
LANES = 128
BLOCKS = WIDTH // LANES
TILE_M = 64
INNER = 13
OUTER = 5
OWN_PATCHES = 4
K = 3072
PAIR = 2
VMEM = 60 * 1024 * 1024
BF = jnp.bfloat16
F32 = jnp.float32


def lane_iota(rows):
    return lax.broadcasted_iota(jnp.int32, (rows, LANES), 1)


def row_choice(picked, row_of):
    shape = (picked * 16, 16 * ROWS)
    out = lax.broadcasted_iota(jnp.int32, shape, 0)
    source = (out & 15) * ROWS + row_of(lax.shift_right_logical(out, 4))
    return jnp.where(source == lax.broadcasted_iota(jnp.int32, shape, 1), 1.0, 0.0).astype(BF)


def choose_rows(choice, field, start, level):
    members = field[pl.ds(start, 16), level].reshape(16 * ROWS, WIDTH)
    return jnp.dot(choice, members, preferred_element_type=F32)


def edges_kernel(wind, field, top, bottom):
    step = pl.program_id(0)
    choice = row_choice(4, lambda r: jnp.where(r < 2, r, r + ROWS - 4))

    @pl.when(step == 0)
    def _():
        for pack, row in ((top, 0), (bottom, ROWS - 1)):
            winds = [
                wind[part, level].astype(F32)[row : row + 1] for part in range(2) for level in range(2)
            ]
            rows = jnp.concatenate(winds + [jnp.zeros((12, WIDTH), F32)], axis=0)
            pack[4 * MINE : 4 * MINE + 16] = rows.astype(BF)

    for group in range(TILE_M // 16):
        for level in range(2):
            rows = choose_rows(choice, field, group * 16, level).astype(BF)
            for i in range(2):
                at = pl.multiple_of((level * 2 + i) * MINE + step * TILE_M + group * 16, 16)
                top[pl.ds(at, 16)] = rows[i * 16 : (i + 1) * 16]
                bottom[pl.ds(at, 16)] = rows[32 + i * 16 : 48 + i * 16]


def edges(winds, field):
    pack = jax.ShapeDtypeStruct((4 * MINE + 16, WIDTH), BF)
    return pl.pallas_call(
        edges_kernel,
        grid=(MINE // TILE_M,),
        in_specs=[
            pl.BlockSpec((2, 2, ROWS, WIDTH), lambda i: (0, 0, 0, 0)),
            pl.BlockSpec((TILE_M, 2, ROWS, WIDTH), lambda i: (i, 0, 0, 0)),
        ],
        out_specs=[pl.BlockSpec(pack.shape, lambda i: (0, 0))] * 2,
        out_shape=[pack] * 2,
        compiler_params=pltpu.CompilerParams(vmem_limit_bytes=VMEM),
        cost_estimate=pl.CostEstimate(flops=10**7, bytes_accessed=10 * 2**20, transcendentals=0),
        name="edges",
    )(winds, field)


def observe_kernel(inner, sc, wind, field, *refs):
    if inner:
        rows = ROWS
    else:
        lows, low_wind = refs[0:4], refs[4]
        highs, high_wind = refs[5:9], refs[9]
        refs = refs[10:]
        rows = 12
    outs = refs[0:4]
    raw, once, coef, row_out, edge = refs[4:]
    me = sc[0]
    lane = lane_iota(TILE_M)
    first = lane_iota(8) == 0
    last = lane_iota(8) == LANES - 1

    @pl.when(pl.program_id(0) == 0)
    def _():
        column = lax.broadcasted_iota(jnp.int32, (1, WIDTH), 1)

        def coefs(a, b):
            up, down = jnp.maximum(a, 0.0), -jnp.minimum(a, 0.0)
            left, right = jnp.maximum(b, 0.0), -jnp.minimum(b, 0.0)
            centre = 1.0 - up - down - left - right
            left = jnp.where(column == 0, 0.0, left)
            right = jnp.where(column == WIDTH - 1, 0.0, right)
            return centre, up, down, left, right

        def put(at_row, level, arrays, r):
            for k, array in enumerate(arrays):
                coef[at_row, level * 5 + k] = jnp.broadcast_to(array[r : r + 1], (8, WIDTH))

        if inner:
            places = [(r, r) for r in range(1, ROWS - 1)]
        else:
            places = [(2, 0), (3, 1), (4, 2), (7, 13), (8, 14), (9, 15)]
        for level in range(2):
            arrays = coefs(wind[0, level].astype(F32), wind[1, level].astype(F32))
            for at_row, r in places:
                put(at_row, level, arrays, r)
            if not inner:
                for side, at_row in ((low_wind, 1), (high_wind, 10)):
                    winds = side[...].astype(F32)
                    put(at_row, level, coefs(winds[level : level + 1], winds[2 + level : 3 + level]), 0)
        row_out[0] = jnp.zeros((TILE_M, LANES), F32)
        row_out[BLOCKS + 1] = jnp.zeros((TILE_M, LANES), F32)

    if inner:
        picked, at_first, choice = ROWS, 0, row_choice(ROWS, lambda r: r)
    else:
        picked, at_first, choice = 8, 2, row_choice(8, lambda r: jnp.where(r < 4, r, r + 8))
        for level in range(2):
            for i in range(2):
                raw[level, i] = lows[level * 2 + i][...].astype(F32)
                raw[level, 10 + i] = highs[level * 2 + i][...].astype(F32)

    def reorder(group, carry):
        start = pl.multiple_of(group * 16, 16)
        for level in range(2):
            chosen = choose_rows(choice, field, start, level)
            for r in range(picked):
                raw[level, at_first + r, pl.ds(start, 16), :] = chosen[r * 16 : (r + 1) * 16]
        return carry

    lax.fori_loop(0, TILE_M // 16, reorder, 0)

    def stencil(src, level, row):
        tiles = range(TILE_M // 8)

        def block(at_row, m, j):
            return src[level, at_row, m * 8 : (m + 1) * 8, j * LANES : (j + 1) * LANES]

        here = [block(row, m, 0) for m in tiles]
        before = [None for m in tiles]
        turned_back = [pltpu.roll(here[m], LANES - 1, 1) for m in tiles]
        for j in range(BLOCKS):
            lanes = slice(j * LANES, (j + 1) * LANES)
            centre, up, down, west, east = (coef[row, level * 5 + k, :, lanes] for k in range(5))
            for m in tiles:
                turned = pltpu.roll(here[m], 1, 1)
                left = turned if j == 0 else jnp.where(first, before[m], turned)
                right = turned_back[m]
                after, after_back = None, None
                if j + 1 < BLOCKS:
                    after = block(row, m, j + 1)
                    after_back = pltpu.roll(after, LANES - 1, 1)
                    right = jnp.where(last, after_back, right)
                value = (
                    centre * here[m]
                    + up * block(row - 1, m, j)
                    + down * block(row + 1, m, j)
                    + west * left
                    + east * right
                )
                yield j, slice(m * 8, (m + 1) * 8), value
                before[m], here[m], turned_back[m] = turned, after, after_back

    def step_one(row, carry):
        for level in range(2):
            for j, members, value in stencil(raw, level, row):
                once[level, row, members, j * LANES : (j + 1) * LANES] = value
        return carry

    def step_two(row, base, slot):
        for j, members, value in stencil(once, 0, row):
            row_out[1 + j, members] = LOW_SHARE * value
        for j, members, value in stencil(once, 1, row):
            row_out[1 + j, members] = row_out[1 + j, members] + HIGH_SHARE * value
        for s in range(GROUPS):
            d = me ^ s
            for j in range(2):
                outs[s][base + j] = row_out[1 + 2 * d + j].astype(BF)
            outer = jnp.where(
                lane < HALO_R,
                row_out[2 * d + 3],
                jnp.where(lane >= LANES - HALO_R, row_out[2 * d], 0.0),
            )
            edge[s] = edge[s] + pltpu.roll(outer, HALO_R + 2 * HALO_R * slot, 1)

    def clear():
        for s in range(GROUPS):
            edge[s] = jnp.zeros((TILE_M, LANES), F32)

    def flush(at):
        for s in range(GROUPS):
            outs[s][at] = edge[s].astype(BF)

    if inner:
        lax.fori_loop(1, ROWS - 1, step_one, 0)
        for half in range(2):
            clear()

            def step(t, carry, half=half):
                step_two(2 + half * 6 + t, half * INNER + 2 * t, t)
                return carry

            lax.fori_loop(0, 6, step, 0)
            flush(half * INNER + 12)
    else:
        lax.fori_loop(1, 5, step_one, 0)
        lax.fori_loop(7, 11, step_one, 0)
        clear()

        def step(t, carry):
            under = t // 2
            step_two(2 + t + 4 * under, 2 * t + under, t)
            return carry

        lax.fori_loop(0, 4, step, 0)
        flush(4)


def observe(inner, scalars, winds, *arrays):
    steps = MINE // TILE_M
    wind_spec = pl.BlockSpec((2, 2, ROWS, WIDTH), lambda i, sc: (0, 0, 0, 0))
    specs = [pl.BlockSpec((TILE_M, 2, ROWS, WIDTH), lambda i, sc: (i, 0, 0, 0))]
    if inner:
        rows, blocks, work = ROWS, 2 * INNER, 7
        operands = arrays
    else:
        rows, blocks, work = 12, 9, 3
        side = [
            pl.BlockSpec((TILE_M, WIDTH), functools.partial(lambda k, i, sc: (k * steps + i, 0), k))
            for k in range(4)
        ] + [pl.BlockSpec((16, WIDTH), lambda i, sc: (4 * MINE // 16, 0))]
        specs = specs + side * 2
        field, low, high = arrays
        operands = [field] + [low] * 5 + [high] * 5
    return pl.pallas_call(
        functools.partial(observe_kernel, inner),
        grid_spec=pltpu.PrefetchScalarGridSpec(
            num_scalar_prefetch=1,
            grid=(steps,),
            in_specs=[wind_spec] + specs,
            out_specs=[pl.BlockSpec((blocks, TILE_M, LANES), lambda i, sc: (0, i, 0))] * GROUPS,
            scratch_shapes=[
                pltpu.VMEM((2, rows, TILE_M, WIDTH), F32),
                pltpu.VMEM((2, rows, TILE_M, WIDTH), F32),
                pltpu.VMEM((rows, 10, 8, WIDTH), F32),
                pltpu.VMEM((BLOCKS + 2, TILE_M, LANES), F32),
                pltpu.VMEM((GROUPS, TILE_M, LANES), F32),
            ],
        ),
        out_shape=[jax.ShapeDtypeStruct((blocks, MINE, LANES), BF)] * GROUPS,
        compiler_params=pltpu.CompilerParams(vmem_limit_bytes=VMEM),
        cost_estimate=pl.CostEstimate(
            flops=10**7, bytes_accessed=work * 10 * 2**20, transcendentals=0
        ),
        name="observe_inner" if inner else "observe_outer",
    )(scalars, winds, *operands)


def weights_kernel(sc, index, precision, values, spread, pull):
    me, grid_at = sc[0], sc[1]
    patch = me * OWN_PATCHES + pl.program_id(0)
    row_low = grid_at * ROWS - HALO_R
    chunk = 512
    total = jnp.zeros((6 * 32, LANES), F32)
    for c in range(K // chunk):
        at = slice(c * chunk, (c + 1) * chunk)
        cell = index[0, :, at]
        row = lax.shift_right_logical(cell, 10) - row_low
        spot = cell & (LANES - 1)
        weight = precision[0, :, at]
        parts = []
        for item in (weight, weight * values[0, :, at]):
            for _ in range(3):
                top = item.astype(BF).astype(F32)
                parts.append(top)
                item = item - top
        in_row = lax.broadcasted_iota(jnp.int32, (32, chunk), 0) == row
        at_spot = lax.broadcasted_iota(jnp.int32, (LANES, chunk), 0) == spot
        left = jnp.concatenate([jnp.where(in_row, part, 0.0) for part in parts], axis=0).astype(BF)
        right = jnp.where(at_spot, 1.0, 0.0).astype(BF)
        total = total + lax.dot_general(
            left, right, (((1,), (1,)), ((), ())), preferred_element_type=F32
        )
    weight_sum = total[0:32] + total[32:64] + total[64:96]
    value_sum = total[96:128] + total[128:160] + total[160:192]
    r = lax.broadcasted_iota(jnp.int32, (32, LANES), 0).astype(F32)
    offset = (lane_iota(32) - patch * PATCH_C + HALO_R) & (LANES - 1)
    row_diff = r - (HALO_R + (ROWS - 1) * 0.5)
    col_diff = offset.astype(F32) - (HALO_R + (PATCH_C - 1) * 0.5)
    distance = row_diff * row_diff + col_diff * col_diff
    share = jnp.exp(-distance / LOC_AREA) / (MEMBERS - 1.0)
    weight_all = weight_sum * share
    root = jnp.sqrt(weight_all)
    seen = weight_all > 0.0
    spread[0] = root
    pull[0] = jnp.where(seen, value_sum * share / jnp.where(seen, root, 1.0), 0.0)


def weigh(scalars, index, precision, values):
    spec = pl.BlockSpec((1, 1, K), lambda p, sc: (p, 0, 0))
    out = pl.BlockSpec((1, 32, LANES), lambda p, sc: (p, 0, 0))
    shape = jax.ShapeDtypeStruct((OWN_PATCHES, 32, LANES), F32)
    spread, pull = pl.pallas_call(
        weights_kernel,
        grid_spec=pltpu.PrefetchScalarGridSpec(
            num_scalar_prefetch=1,
            grid=(OWN_PATCHES,),
            in_specs=[spec] * 3,
            out_specs=[out] * 2,
        ),
        out_shape=[shape] * 2,
        compiler_params=pltpu.CompilerParams(vmem_limit_bytes=VMEM),
        cost_estimate=pl.CostEstimate(flops=10**9, bytes_accessed=2**18, transcendentals=0),
        name="weigh",
    )(
        scalars,
        index.reshape(OWN_PATCHES, 1, K),
        precision.reshape(OWN_PATCHES, 1, K),
        values.reshape(OWN_PATCHES, 1, K),
    )
    return spread, pull


def own_plan():
    return [
        [(half * INNER + 2 * t, half * INNER + 12, t, 10 + 6 * half + t) for t in range(6)]
        for half in range(2)
    ]


def inner_plan():
    return [
        [(2 * t, 12, t, t) for t in range(6)],
        [(INNER + 2 * t, INNER + 12, t, 26 + t) for t in range(6)],
    ]


def outer_plan():
    rows = [(2 * t, 4, t, 8 + t) for t in range(2)]
    rows += [(5 + 2 * t, 4, 2 + t, 22 + t) for t in range(2)]
    halo = [(10 + 2 * t, 9, 2 + t, 6 + t) for t in range(2)]
    halo += [(14 + 2 * t, 18, t, 24 + t) for t in range(2)]
    return [rows, halo]


def gram_rows(plan, patches, spread, pull, cells, scaled, mean_of, total):
    lane_row = lane_iota(1)
    lane = lane_iota(MINE)
    at_top = lax.broadcasted_iota(jnp.int32, (16, LANES), 0) == 0

    def pick(p, first, second, outer, lanes):
        low_edge = lanes < HALO_R
        high_edge = lanes >= LANES - HALO_R
        if p == 0:
            return jnp.where(high_edge, outer, first)
        if p == 1:
            return jnp.where(low_edge, second, first)
        if p == 2:
            return jnp.where(high_edge, first, second)
        return jnp.where(low_edge, outer, second)

    ones = jnp.full((8, MEMBERS), 1.0, BF)
    used = set()
    for chunk in plan:
        for at, edge_at, _, _ in chunk:
            used |= {at, at + 1, edge_at}
    for at in sorted(used):
        summed = jnp.dot(
            ones, cells[at].reshape(MEMBERS, LANES), preferred_element_type=F32
        )
        mean_of[at] = summed / MEMBERS

    def multiply(c, i, width):
        total[i] = total[i] + lax.dot_general(
            scaled[c, i, :, 0:width],
            scaled[c, i, 0:MEMBERS, 0:width],
            (((1,), (1,)), ((), ())),
            preferred_element_type=F32,
        )

    waiting = []
    for c, chunk in enumerate(plan):
        for n, (at, edge_at, slot, window_row) in enumerate(chunk):
            back = LANES - HALO_R - 2 * HALO_R * slot
            outer_mean = pltpu.roll(mean_of[edge_at], back, 1)[0:1]
            first_mean, second_mean = mean_of[at, 0:1, :], mean_of[at + 1, 0:1, :]
            place = slice(n * LANES, (n + 1) * LANES)
            means, roots = [], []
            for i, p in enumerate(patches):
                mean = pick(p, first_mean, second_mean, outer_mean, lane_row)
                root = spread[p, window_row : window_row + 1, :]
                innov = pull[p, window_row : window_row + 1, :] - root * mean
                scaled[c, i, MEMBERS : MEMBERS + 16, place] = jnp.where(at_top, innov, 0.0).astype(BF)
                means.append(mean)
                roots.append(root)
            for group in range(GROUPS):
                first = cells[at, group].astype(F32)
                second = cells[at + 1, group].astype(F32)
                outer = pltpu.roll(cells[edge_at, group].astype(F32), back, 1)
                for i, p in enumerate(patches):
                    picked = pick(p, first, second, outer, lane)
                    scaled[c, i, group * MINE : (group + 1) * MINE, place] = (
                        (picked - means[i]) * roots[i]
                    ).astype(BF)
            if waiting:
                multiply(*waiting.pop(0))
        for ready in waiting:
            multiply(*ready)
        waiting = [(c, i, len(chunk) * LANES) for i in range(len(patches))]
    for ready in waiting:
        multiply(*ready)


def fetch_all(moves, cells, sems):
    copies = []
    for n, (src, at, count, group) in enumerate(moves):
        copy = pltpu.make_async_copy(src, cells.at[pl.ds(at, count), group], sems.at[n])
        copy.start()
        copies.append(copy)
    for copy in copies:
        copy.wait()


def own_kernel(sc, spread, pull, *refs):
    pieces, totals = refs[0:4], refs[4:6]
    cells, scaled, mean_of, total, sems = refs[6:]
    me = sc[0]
    fetch_all([(pieces[s], 0, 2 * INNER, me ^ s) for s in range(GROUPS)], cells, sems)
    total[...] = jnp.zeros_like(total)
    gram_rows(own_plan(), list(range(OWN_PATCHES)), spread, pull, cells, scaled, mean_of, total)
    for i in range(OWN_PATCHES):
        totals[i // PAIR][i % PAIR] = total[i]


def inner_kernel(sc, spread, pull, *refs):
    before, near, far, totals = refs[0:2], refs[2:4], refs[4:6], refs[6:8]
    cells, scaled, mean_of, total, sems = refs[8:]
    me = sc[0]
    moves = []
    for side in range(2):
        for s in range(GROUPS):
            moves.append(((near, far)[s // 2][side].at[s % 2], side * INNER, INNER, me ^ s))
    fetch_all(moves, cells, sems)
    for i in range(OWN_PATCHES):
        total[i] = before[i // PAIR][i % PAIR]
    gram_rows(inner_plan(), list(range(OWN_PATCHES)), spread, pull, cells, scaled, mean_of, total)
    for i in range(OWN_PATCHES):
        totals[i // PAIR][i % PAIR] = total[i]


def running_gram(kernel, name, scalars, spread, pull, before, pieces):
    vmem = pl.BlockSpec(memory_space=pltpu.VMEM)
    anywhere = pl.BlockSpec(memory_space=pl.ANY)
    return pl.pallas_call(
        kernel,
        in_specs=[pl.BlockSpec(memory_space=pltpu.SMEM)]
        + [vmem] * (2 + len(before))
        + [anywhere] * len(pieces),
        out_specs=[vmem] * 2,
        out_shape=[jax.ShapeDtypeStruct((PAIR, MEMBERS + 16, MEMBERS), F32)] * 2,
        scratch_shapes=[
            pltpu.VMEM((2 * INNER, GROUPS, MINE, LANES), BF),
            pltpu.VMEM((2, OWN_PATCHES, MEMBERS + 16, 6 * LANES), BF),
            pltpu.VMEM((2 * INNER, 8, LANES), F32),
            pltpu.VMEM((OWN_PATCHES, MEMBERS + 16, MEMBERS), F32),
            pltpu.SemaphoreType.DMA((8,)),
        ],
        compiler_params=pltpu.CompilerParams(vmem_limit_bytes=VMEM),
        cost_estimate=pl.CostEstimate(flops=10**7, bytes_accessed=35 * 2**20, transcendentals=0),
        name=name,
    )(scalars, spread, pull, *before, *pieces)


def last_kernel(patches, sc, spread, pull, before, *refs):
    own, low, high, outs = refs[0:4], refs[4], refs[5], refs[6:10]
    cells, scaled, mean_of, total, sems = refs[10:]
    me = sc[0]
    moves = []
    for s in range(GROUPS):
        moves.append((own[s].at[pl.ds(0, 9)], 0, 9, me ^ s))
        moves.append((low.at[s], 9, OUTER, me ^ s))
        moves.append((high.at[s], 14, OUTER, me ^ s))
    fetch_all(moves, cells, sems)
    total[...] = before[...]
    gram_rows(outer_plan(), patches, spread, pull, cells, scaled, mean_of, total)
    for i in range(PAIR):
        for s in range(GROUPS):
            at = pl.multiple_of((me ^ s) * MINE, MINE)
            projected = total[i, MEMBERS : MEMBERS + 8, pl.ds(at, MINE)]
            top = projected.astype(BF).astype(F32)
            zero = jnp.zeros_like(top)
            extra = jnp.concatenate([top, projected - top, zero, zero], axis=1)
            block = total[i, pl.ds(at, MINE), :]
            if s == 0:
                outs[s][i, 0:MINE, :] = block
                outs[s][i, MINE : MINE + 8, :] = extra
            else:
                outs[s][i, 0:MINE, :] = block.astype(BF)
                outs[s][i, MINE : MINE + 16, :] = jnp.concatenate([extra, extra], axis=0).astype(BF)


def last_gram(patches, scalars, spread, pull, before, own, low, high):
    vmem = pl.BlockSpec(memory_space=pltpu.VMEM)
    anywhere = pl.BlockSpec(memory_space=pl.ANY)
    return pl.pallas_call(
        functools.partial(last_kernel, patches),
        in_specs=[pl.BlockSpec(memory_space=pltpu.SMEM), vmem, vmem, vmem] + [anywhere] * 6,
        out_specs=[vmem] * GROUPS,
        out_shape=[jax.ShapeDtypeStruct((PAIR, MINE + 8, MEMBERS), F32)]
        + [jax.ShapeDtypeStruct((PAIR, MINE + 16, MEMBERS), BF)] * (GROUPS - 1),
        scratch_shapes=[
            pltpu.VMEM((19, GROUPS, MINE, LANES), BF),
            pltpu.VMEM((2, PAIR, MEMBERS + 16, 4 * LANES), BF),
            pltpu.VMEM((19, 8, LANES), F32),
            pltpu.VMEM((PAIR, MEMBERS + 16, MEMBERS), F32),
            pltpu.SemaphoreType.DMA((12,)),
        ],
        compiler_params=pltpu.CompilerParams(vmem_limit_bytes=VMEM),
        cost_estimate=pl.CostEstimate(flops=10**7, bytes_accessed=30 * 2**20, transcendentals=0),
        name=f"gram_last_{patches[0]}",
    )(scalars, spread, pull, before, *own, low, high)


def assemble_kernel(which, sc, *refs):
    gram, proj = refs[-2], refs[-1]
    for n, s in enumerate(which):

        @pl.when(pl.program_id(0) == n)
        def _(n=n, s=s):
            for p in range(PAIR):
                gram[p] = refs[n][p, 0:MINE, :].astype(F32)
                extra = refs[n][p, MINE : MINE + (8 if s == 0 else 16), :].astype(F32)
                proj[0, p : p + 1, :] = extra[0:1, 0:MINE] + extra[0:1, MINE : 2 * MINE]


def assemble(half, which, scalars, parts, begun):
    def at(n, sc):
        return ((sc[0] ^ (n + which[0])) * 2 + half, 0, 0)

    begun = [] if begun is None else list(begun)
    count = len(which)
    return pl.pallas_call(
        functools.partial(assemble_kernel, which),
        grid_spec=pltpu.PrefetchScalarGridSpec(
            num_scalar_prefetch=1,
            grid=(count,),
            in_specs=[pl.BlockSpec(parts[s].shape, lambda n, sc: (0, 0, 0)) for s in which]
            + [pl.BlockSpec(memory_space=pl.ANY)] * len(begun),
            out_specs=[
                pl.BlockSpec((PAIR, MINE, MEMBERS), at),
                pl.BlockSpec((1, PAIR, MINE), at),
            ],
        ),
        out_shape=[
            jax.ShapeDtypeStruct((GROUPS * OWN_PATCHES, MINE, MEMBERS), F32),
            jax.ShapeDtypeStruct((2 * GROUPS, PAIR, MINE), F32),
        ],
        input_output_aliases={count + 1: 0, count + 2: 1} if begun else {},
        compiler_params=pltpu.CompilerParams(vmem_limit_bytes=VMEM),
        cost_estimate=pl.CostEstimate(flops=10**6, bytes_accessed=count * 2**20, transcendentals=0),
        name=f"assemble_{half}_{which[0]}",
    )(scalars, *[parts[s] for s in which], *begun)


def bundle_kernel(plan, count, arrays, *refs):
    sources, outs, sems = refs[:arrays], refs[arrays : arrays + 2], refs[arrays + 2]
    copies = []
    for out, starts in zip(outs, plan):
        for k, start in enumerate(starts):
            source = sources[k].at[pl.ds(start, count)]
            copies.append(pltpu.make_async_copy(source, out.at[k], sems.at[len(copies)]))
    for copy in copies:
        copy.start()
    for copy in copies:
        copy.wait()


def bundle(name, pieces, count, low_start, high_start):
    n = len(pieces)
    plan = ([low_start] * n, [high_start] * n)
    anywhere = pl.BlockSpec(memory_space=pl.ANY)
    return pl.pallas_call(
        functools.partial(bundle_kernel, plan, count, n),
        in_specs=[anywhere] * n,
        out_specs=[pl.BlockSpec(memory_space=pltpu.VMEM)] * 2,
        out_shape=[jax.ShapeDtypeStruct((n, count, MINE, LANES), BF)] * 2,
        scratch_shapes=[pltpu.SemaphoreType.DMA((2 * n,))],
        compiler_params=pltpu.CompilerParams(vmem_limit_bytes=VMEM),
        cost_estimate=pl.CostEstimate(flops=0, bytes_accessed=4 * 2**20, transcendentals=0),
        name=name,
    )(*pieces)


def after(*arrays):
    return lax.optimization_barrier(arrays)


def per_device(field, winds, obs_index, measured_values, precision_weights):
    grid_size = lax.axis_size("grid")
    me = lax.axis_index("mem")
    scalars = jnp.stack([me, lax.axis_index("grid")]).astype(jnp.int32)
    forward = [(i, i + 1) for i in range(grid_size - 1)]
    backward = [(i + 1, i) for i in range(grid_size - 1)]

    def swap(x, s):
        return lax.ppermute(x, "mem", [(i, i ^ s) for i in range(GROUPS)])

    def exchange(pieces):
        far = [swap(pieces[s], s) for s in (2, 3)]
        return [pieces[0], swap(pieces[1], 1)] + far

    top, bottom = edges(winds, field)
    low = lax.ppermute(bottom, "grid", forward)
    high = lax.ppermute(top, "grid", backward)

    inner = observe(True, scalars, winds, field)
    low, high, *inner = after(low, high, *inner)
    far_inner = [swap(inner[s], s) for s in (2, 3)]
    near_inner = [inner[0], swap(inner[1], 1)]
    near_up, near_down = bundle("bundle_near", near_inner, INNER, INNER, 0)
    near_up, near_down, low, obs_index, measured_values, precision_weights = after(
        near_up, near_down, low, obs_index, measured_values, precision_weights
    )
    near_low = lax.ppermute(near_up, "grid", forward)
    near_high = lax.ppermute(near_down, "grid", backward)

    outer = observe(False, scalars, winds, field, low, high)

    def mine(x):
        return lax.dynamic_slice_in_dim(x, me * OWN_PATCHES, OWN_PATCHES, 0)

    spread, pull = weigh(scalars, mine(obs_index), mine(precision_weights), mine(measured_values))

    far_inner[0], far_inner[1], spread, pull, *outer = after(*far_inner, spread, pull, *outer)
    far_up, far_down = bundle("bundle_far", far_inner, INNER, INNER, 0)
    totals = running_gram(
        own_kernel, "gram_own", scalars, spread, pull, [], near_inner + far_inner
    )
    near_low, near_high, far_up, far_down, *rest = after(
        near_low, near_high, far_up, far_down, *totals, *outer
    )
    totals, outer = rest[:2], rest[2:]
    far_outer = [swap(outer[s], s) for s in (2, 3)]
    far_up, far_down, core_outer = after(far_up, far_down, swap(outer[1], 1))
    outer = [outer[0], core_outer] + far_outer
    far_low = lax.ppermute(far_up, "grid", forward)
    far_high = lax.ppermute(far_down, "grid", backward)
    outer_up, outer_down = bundle("bundle_outer", outer, OUTER, 4, 0)
    outer_low = lax.ppermute(outer_up, "grid", forward)
    outer_high = lax.ppermute(outer_down, "grid", backward)

    halos = [near_low, near_high, far_low, far_high]
    totals = running_gram(
        inner_kernel, "gram_inner", scalars, spread, pull, totals, halos
    )
    result = None
    for n in range(2):
        patches = [PAIR * n, PAIR * n + 1]
        sent = last_gram(
            patches, scalars, spread, pull, totals[n], outer, outer_low, outer_high
        )
        parts = exchange(sent)
        for which in ([0, 1, 2, 3],) if n == 0 else ([0, 1], [2], [3]):
            result = assemble(n, which, scalars, parts, result)
    return result[0], result[1].reshape(GROUPS * OWN_PATCHES, MINE)


def solution(mesh):
    return jax.shard_map(
        per_device,
        mesh=mesh,
        in_specs=(
            P("mem", None, "grid", None),
            P(None, None, "grid", None),
            P("grid", None),
            P("grid", None),
            P("grid", None),
        ),
        out_specs=(P("grid", "mem", None), P("grid", "mem")),
        check_vma=False,
    )
```

time: 1270 us -> 201 us (0.16)
  local copies, waits for them, and re-layouts: 666 us -> 9.38 us
  waiting for transfers between devices: 335 us -> 24.4 us
  other arithmetic: 189 us -> 0.61 us
  Pallas kernels: 0 us -> 109 us
  starting transfers between devices: 30 us -> 55.2 us
  matrix products: 25 us -> 0 us
  between operations: 14.2 us -> 0.89 us
    gather x16 -> x0, local copies, waits for them, and re-layouts: 564 us -> none  [one_patch(): seen = jnp.take(flat, index, axis=0)]
    ppermute x6 -> x20, waiting for transfers between devices: 221 us -> 24.4 us  [the longest x12 9.91 us: swap(): return lax.ppermute(x, 'mem', [(i, i ^ s) for i in range(GROUPS)])]
    all_gather x1 -> x0, waiting for transfers between devices: 114 us -> none  [per_device(): everyone = lax.all_gather(cellwise, 'mem', axis=2, tiled=True)]
    pallas_call x0 -> x15, Pallas kernels: none -> 109 us  [the longest x2 45.1 us: observe(): pl.pallas_call(functools.partial(observe_kernel, inner), grid_spec=pltpu....]
    sub x2 -> x0, other arithmetic: 65.6 us -> none  [advect_rows(): middle - jnp.maximum(flow_rows, 0.0) * (middle - above)]
    convert_element_type x35 -> x0, other arithmetic: 64.3 us -> none  [the longest x16 43 us: one_patch(): (root_patch[:, None] * (seen.astype(jnp.float32) - mean[:, None])).astype...]
    while x1 -> x0, local copies, waits for them, and re-layouts: 45.5 us -> none  [per_device(): gram, proj = lax.map(one_patch, (nearby_index, root, measured_values))]
    reduce_sum x16 -> x0, other arithmetic: 34.2 us -> none  [one_patch(): mean = jnp.sum(seen.astype(jnp.float32), axis=1) / members]
  transfers between devices with their start and end apart: 7 -> 20, of which waited for: 7 -> 7; matrix products, arithmetic and copies ran while one was open for 0% -> 2% of each run, Pallas kernels for 0% -> 47%
where the time goes in v1:
time: 201 us; the launch traced here: 200 us
  Pallas kernels  109 us (54%)
  starting transfers between devices  55.2 us (27%)
  waiting for transfers between devices  24.4 us (12%)
  local copies, waits for them, and re-layouts  9.38 us (5%)
    pallas_call x2, Pallas kernels, observe(): pl.pallas_call(functools.partial(observe_kernel, inner), grid_spec=pltpu....  45.1 us
    pallas_call x2, Pallas kernels, running_gram(): pl.pallas_call(kernel, in_specs=[pl.BlockSpec(memory_space=pltpu.SMEM)] +...  21.2 us
    ppermute x12, starting transfers between devices, swap(): return lax.ppermute(x, 'mem', [(i, i ^ s) for i in range(GROUPS)])  16.7 us
    pallas_call x2, Pallas kernels, last_gram(): pl.pallas_call(functools.partial(last_kernel, patches), in_specs=[pl.Bloc...  13.3 us
    pallas_call x4, Pallas kernels, assemble(): pl.pallas_call(functools.partial(assemble_kernel, which), grid_spec=pltpu...  11.6 us
    ppermute x12, waiting for transfers between devices, swap(): return lax.ppermute(x, 'mem', [(i, i ^ s) for i in range(GROUPS)])  9.91 us
    pallas_call x3, Pallas kernels, bundle(): pl.pallas_call(functools.partial(bundle_kernel, plan, count, n), in_specs...  7.86 us
    ppermute x1, starting transfers between devices, per_device(): near_high = lax.ppermute(near_down, 'grid', backward)  7.58 us
  transfers between devices with their start and end apart: 20, of which 7 were waited for; matrix products, arithmetic and copies ran while one was open for 2% of the time, Pallas kernels for 47%

profile of v1, /device:TPU:3, one launch (start us, length us, event | category | flops | bytes accessed | tf_op | source)
XLA Modules:
  0.0 199.7 jit_solution(12425285021646414612)
XLA Ops:
  0.6 0.0 copy-start
  0.6 5.8 %edges.1 = (bf16[528,1024]{1,0:T(8,128)(2,1)}, bf16[528,1024]{1,0:T(8,128)(2,1)}) custom-call(bf16[2,2,16,1024]{3,2,1,0:T(8,128)(2,1)} %wind.5, bf16[128,2,16,1024]{3,2,1,0:T(8,128)(2,1)} %field.5), custom_call_target="tpu_custom_call" | custom-call | flops 10000000 | bytes 10485760 | tf_op jit(solution)/shard_map/edges/pallas_call | solution.py:74
  6.4 3.2 %collective-permute-start = (bf16[528,1024]{1,0:T(8,128)(2,1)}, bf16[528,1024]{1,0:T(8,128)(2,1)S(1)}, u32[]{:S(2)}, u32[]{:S(2)}) collective-permute-start(bf16[528,1024]{1,0:T(8,128)(2,1)} %get-tuple-element.73), channel_id=1, source_target_pairs={{0,4},{4,8},{8,12},{12,16},{16,20},{20,24},{24,28},{28,32},{32,36}... | collective-permute-start | bytes 3244040 | tf_op jit(solution)/shard_map/ppermute | solution.py:634
  9.6 6.8 %collective-permute-start.1 = (bf16[528,1024]{1,0:T(8,128)(2,1)}, bf16[528,1024]{1,0:T(8,128)(2,1)S(1)}, u32[]{:S(2)}, u32[]{:S(2)}) collective-permute-start(bf16[528,1024]{1,0:T(8,128)(2,1)} %get-tuple-element.74), channel_id=1, source_target_pairs={{4,0},{8,4},{12,8},{16,12},{20,16},{24,20},{28,24},{32,28},{36,32}... | collective-permute-start | bytes 3244040 | tf_op jit(solution)/shard_map/ppermute | solution.py:635
  16.4 0.6 pad_add_fusion.sc
  17.0 28.7 %observe_inner.1 = (bf16[26,128,128]{2,1,0:T(8,128)(2,1)}, bf16[26,128,128]{2,1,0:T(8,128)(2,1)}, bf16[26,128,128]{2,1,0:T(8,128)(2,1)}, bf16[26,128,128]{2,1,0:T(8,128)(2,1)}) custom-call(s32[2]{0:T(128)} %pad_add_fusion.sc, bf16[2,2,16,1024]{3,2,1,0:T(8,128)(2,1)} %wind.5, bf16[128,2,16,1024]{3,2,1,0:T(8,128)(2,1)} %field.5), custom_call_target="tpu_custom_call" | custom-call | flops 10000000 | bytes 73400320 | tf_op jit(solution)/shard_map/observe_inner/pallas_call | solution.py:256
  45.7 0.0 collective-permute-done.refs_0_.refs_1_.refs_2_.refs_3_.refs_4_
  45.7 0.0 collective-permute-done.1.refs_5_.refs_6_.refs_7_.refs_8_.refs_9_
  45.7 0.0 copy-start.2
  45.7 1.0 collective-permute-start.4
  46.8 2.2 %collective-permute-start.2 = (bf16[26,128,128]{2,1,0:T(8,128)(2,1)}, bf16[26,128,128]{2,1,0:T(8,128)(2,1)}, u32[]{:S(2)}, u32[]{:S(2)}) collective-permute-start(bf16[26,128,128]{2,1,0:T(8,128)(2,1)} %get-tuple-element.79), channel_id=1, source_target_pairs={{0,2},{1,3},{2,0},{3,1},{4,6},{5,7},{6,4},{7,5},{8,10},{9,11},{10,... | collective-permute-start | bytes 2555912 | tf_op jit(solution)/shard_map/ppermute | solution.py:627
  48.9 1.1 collective-permute-start.3
  50.0 0.9 copy-done.3
  50.9 2.7 %bundle_near.1 = (bf16[2,13,128,128]{3,2,1,0:T(8,128)(2,1)}, bf16[2,13,128,128]{3,2,1,0:T(8,128)(2,1)}) custom-call(bf16[26,128,128]{2,1,0:T(8,128)(2,1)} %get-tuple-element.81.refs_0_, bf16[26,128,128]{2,1,0:T(8,128)(2,1)} %copy-done.3), custom_call_target="tpu_custom_call" | custom-call | bytes 4194304 | tf_op jit(solution)/shard_map/bundle_near/pallas_call | solution.py:603
  53.6 1.9 collective-permute-start.5
  55.5 7.6 %collective-permute-start.6 = (bf16[2,13,128,128]{3,2,1,0:T(8,128)(2,1)}, bf16[2,13,128,128]{3,2,1,0:T(8,128)(2,1)}, u32[]{:S(2)}, u32[]{:S(2)}) collective-permute-start(bf16[2,13,128,128]{3,2,1,0:T(8,128)(2,1)} %get-tuple-element.100), channel_id=1, source_target_pairs={{4,0},{8,4},{12,8},{16,12},{20,16},{24,20},{28,24},{32,28},{36,32}... | collective-permute-start | bytes 2555912 | tf_op jit(solution)/shard_map/ppermute | solution.py:646
  63.2 0.6 reshape.16.index
  63.8 1.0 constant_dynamic-slice_fusion
  64.8 0.6 reshape.18.values
  65.4 0.7 reshape.17.precision
  66.1 16.4 %observe_outer.1 = (bf16[9,128,128]{2,1,0:T(8,128)(2,1)}, bf16[9,128,128]{2,1,0:T(8,128)(2,1)}, bf16[9,128,128]{2,1,0:T(8,128)(2,1)}, bf16[9,128,128]{2,1,0:T(8,128)(2,1)}) custom-call(s32[2]{0:T(128)} %pad_add_fusion.sc, bf16[2,2,16,1024]{3,2,1,0:T(8,128)(2,1)} %wind.5, bf16[128,2,16,1024]{3,2,1,0:T(8,128)(2,1)} %field.5, bf16[528,1024]{1,0:T(8,128)(2,1)} %copy-done.1, ...), custom_call_target="tpu_custom_call" | custom-call | flops 10000000 | bytes 31457280 | tf_op jit(solution)/shard_map/observe_outer/pallas_call | solution.py:256
  82.5 4.3 %weigh.1 = (f32[4,32,128]{2,1,0:T(8,128)}, f32[4,32,128]{2,1,0:T(8,128)}) custom-call(s32[2]{0:T(128)} %pad_add_fusion.sc, s32[4,1,3072]{2,1,0:T(1,128)} %reshape.16.index, f32[4,1,3072]{2,1,0:T(1,128)} %reshape.17.precision, f32[4,1,3072]{2,1,0:T(1,128)} %reshape.18.values), custom_call_target="tpu_custom_call" | custom-call | flops 1000000000 | bytes 262144 | tf_op jit(solution)/shard_map/weigh/pallas_call | solution.py:324
  86.9 0.0 collective-permute-done.2.refs_0_.refs_2_
  86.9 1.1 collective-permute-done.3.refs_1_.refs_3_
  88.0 2.6 %bundle_far.1 = (bf16[2,13,128,128]{3,2,1,0:T(8,128)(2,1)}, bf16[2,13,128,128]{3,2,1,0:T(8,128)(2,1)}) custom-call(bf16[26,128,128]{2,1,0:T(8,128)(2,1)} %collective-permute-done.2.refs_0_.refs_2_, bf16[26,128,128]{2,1,0:T(8,128)(2,1)} %collective-permute-done.3.refs_1_.refs_3_), custom_call_target="tpu_custom_call" | custom-call | bytes 4194304 | tf_op jit(solution)/shard_map/bundle_far/pallas_call | solution.py:603
  90.7 9.9 %gram_own.1 = (f32[2,528,512]{2,1,0:T(8,128)}, f32[2,528,512]{2,1,0:T(8,128)}) custom-call(s32[2]{0:T(128)} %pad_add_fusion.sc, f32[4,32,128]{2,1,0:T(8,128)} %get-tuple-element.97.spread, f32[4,32,128]{2,1,0:T(8,128)} %get-tuple-element.98.pull, bf16[26,128,128]{2,1,0:T(8,128)(2,1)} %get-tuple-element.81.refs_0_, bf16[26,128,128]{2,1,0:T(8,128)(2,1)} %copy-done.3, ...), custom_call_target="tpu_custom_call" | custom-call | flops 10000000 | bytes 36700160 | tf_op jit(solution)/shard_map/gram_own/pallas_call | solution.py:475
  100.6 6.4 %collective-permute-done.5.refs_2_ = bf16[2,13,128,128]{3,2,1,0:T(8,128)(2,1)S(1)} collective-permute-done((bf16[2,13,128,128]{3,2,1,0:T(8,128)(2,1)}, bf16[2,13,128,128]{3,2,1,0:T(8,128)(2,1)S(1)}, u32[]{:S(2)}, u32[]{:S(2)}) %collective-permute-start.5) | collective-permute-done | bytes 852000 | tf_op jit(solution)/shard_map/ppermute | solution.py:645
  107.0 0.0 collective-permute-done.6.refs_3_
  107.0 1.0 collective-permute-start.7
  108.0 0.0 collective-permute-start.10
  108.0 3.4 %collective-permute-start.11 = (bf16[9,128,128]{2,1,0:T(8,128)(2,1)S(1)}, bf16[9,128,128]{2,1,0:T(8,128)(2,1)S(1)}, u32[]{:S(2)}, u32[]{:S(2)}) collective-permute-start(bf16[9,128,128]{2,1,0:T(8,128)(2,1)S(1)} %copy-done.17), channel_id=1, source_target_pairs={{0,3},{1,2},{2,1},{3,0},{4,7},{5,6},{6,5},{7,4},{8,11},{9,10},{10,... | collective-permute-start | bytes 884744 | tf_op jit(solution)/shard_map/ppermute | solution.py:627
  111.4 1.9 collective-permute-start.8
  113.3 7.6 %collective-permute-start.9 = (bf16[2,13,128,128]{3,2,1,0:T(8,128)(2,1)}, bf16[2,13,128,128]{3,2,1,0:T(8,128)(2,1)}, u32[]{:S(2)}, u32[]{:S(2)}) collective-permute-start(bf16[2,13,128,128]{3,2,1,0:T(8,128)(2,1)} %get-tuple-element.119), channel_id=1, source_target_pairs={{4,0},{8,4},{12,8},{16,12},{20,16},{24,20},{28,24},{32,28},{36,32}... | collective-permute-start | bytes 2555912 | tf_op jit(solution)/shard_map/ppermute | solution.py:668
  120.9 4.3 %collective-permute-done.11.refs_3_ = bf16[9,128,128]{2,1,0:T(8,128)(2,1)S(1)} collective-permute-done((bf16[9,128,128]{2,1,0:T(8,128)(2,1)S(1)}, bf16[9,128,128]{2,1,0:T(8,128)(2,1)S(1)}, u32[]{:S(2)}, u32[]{:S(2)}) %collective-permute-start.11) | collective-permute-done | bytes 294944 | tf_op jit(solution)/shard_map/ppermute | solution.py:627
  125.2 0.7 copy-done.6
  125.9 2.5 %bundle_outer.1 = (bf16[4,5,128,128]{3,2,1,0:T(8,128)(2,1)}, bf16[4,5,128,128]{3,2,1,0:T(8,128)(2,1)}) custom-call(bf16[9,128,128]{2,1,0:T(8,128)(2,1)} %get-tuple-element.121.refs_0_, bf16[9,128,128]{2,1,0:T(8,128)(2,1)} %copy-done.4, bf16[9,128,128]{2,1,0:T(8,128)(2,1)} %copy-done.5, bf16[9,128,128]{2,1,0:T(8,128)(2,1)} %copy-done.6), custom_call_target="tpu_custom_call" | custom-call | bytes 4194304 | tf_op jit(solution)/shard_map/bundle_outer/pallas_call | solution.py:603
  128.5 1.9 collective-permute-start.12
  130.4 7.6 %collective-permute-start.13 = (bf16[4,5,128,128]{3,2,1,0:T(8,128)(2,1)}, bf16[4,5,128,128]{3,2,1,0:T(8,128)(2,1)S(1)}, u32[]{:S(2)}, u32[]{:S(2)}) collective-permute-start(bf16[4,5,128,128]{3,2,1,0:T(8,128)(2,1)} %get-tuple-element.126), channel_id=1, source_target_pairs={{4,0},{8,4},{12,8},{16,12},{20,16},{24,20},{28,24},{32,28},{36,32}... | collective-permute-start | bytes 1966088 | tf_op jit(solution)/shard_map/ppermute | solution.py:671
  138.0 6.2 %collective-permute-done.8.refs_4_ = bf16[2,13,128,128]{3,2,1,0:T(8,128)(2,1)S(1)} collective-permute-done((bf16[2,13,128,128]{3,2,1,0:T(8,128)(2,1)}, bf16[2,13,128,128]{3,2,1,0:T(8,128)(2,1)S(1)}, u32[]{:S(2)}, u32[]{:S(2)}) %collective-permute-start.8) | collective-permute-done | bytes 852000 | tf_op jit(solution)/shard_map/ppermute | solution.py:667
  144.2 0.0 collective-permute-done.9.refs_5_
  144.2 0.9 copy-done.10
  145.1 11.3 %gram_inner.1 = (f32[2,528,512]{2,1,0:T(8,128)}, f32[2,528,512]{2,1,0:T(8,128)}) custom-call(s32[2]{0:T(128)} %pad_add_fusion.sc, f32[4,32,128]{2,1,0:T(8,128)} %get-tuple-element.97.spread, f32[4,32,128]{2,1,0:T(8,128)} %get-tuple-element.98.pull, f32[2,528,512]{2,1,0:T(8,128)} %get-tuple-element.111.refs_0_, f32[2,528,512]{2,1,0:T(8,128)} %get-tuple-element.112.refs_1_, ...), custom_call_target="tpu_custom_call" | custom-call | flops 10000000 | bytes 36700160 | tf_op jit(solution)/shard_map/gram_inner/pallas_call | solution.py:475
  156.4 1.9 collective-permute-done.12.refs_4_
  158.3 0.8 copy-done.7
  159.1 0.2 copy-done.8
  159.3 6.7 %gram_last_0.1 = (f32[2,136,512]{2,1,0:T(8,128)}, bf16[2,144,512]{2,1,0:T(8,128)(2,1)}, bf16[2,144,512]{2,1,0:T(8,128)(2,1)}, bf16[2,144,512]{2,1,0:T(8,128)(2,1)}) custom-call(s32[2]{0:T(128)} %pad_add_fusion.sc, f32[4,32,128]{2,1,0:T(8,128)} %get-tuple-element.97.spread, f32[4,32,128]{2,1,0:T(8,128)} %get-tuple-element.98.pull, ...), custom_call_target="tpu_custom_call" | custom-call | flops 10000000 | bytes 31457280 | tf_op jit(solution)/shard_map/gram_last_0/pallas_call | solution.py:526
  166.0 1.2 collective-permute-start.17
  167.2 1.0 collective-permute-start.18
  168.1 2.3 %collective-permute-start.19 = (bf16[2,144,512]{2,1,0:T(8,128)(2,1)}, bf16[2,144,512]{2,1,0:T(8,128)(2,1)S(1)}, u32[]{:S(2)}, u32[]{:S(2)}) collective-permute-start(bf16[2,144,512]{2,1,0:T(8,128)(2,1)} %get-tuple-element.135), channel_id=1, source_target_pairs={{0,3},{1,2},{2,1},{3,0},{4,7},{5,6},{6,5},{7,4},{8,11},{9,10},{10,... | collective-permute-start | bytes 884744 | tf_op jit(solution)/shard_map/ppermute | solution.py:627
  170.4 6.7 %gram_last_2.1 = (f32[2,136,512]{2,1,0:T(8,128)}, bf16[2,144,512]{2,1,0:T(8,128)(2,1)}, bf16[2,144,512]{2,1,0:T(8,128)(2,1)}, bf16[2,144,512]{2,1,0:T(8,128)(2,1)}) custom-call(s32[2]{0:T(128)} %pad_add_fusion.sc, f32[4,32,128]{2,1,0:T(8,128)} %get-tuple-element.97.spread, f32[4,32,128]{2,1,0:T(8,128)} %get-tuple-element.98.pull, ...), custom_call_target="tpu_custom_call" | custom-call | flops 10000000 | bytes 31457280 | tf_op jit(solution)/shard_map/gram_last_2/pallas_call | solution.py:526
  177.1 0.2 collective-permute-start.16
  177.3 1.0 collective-permute-start.15
  178.3 0.0 collective-permute-done.17.refs_1_
  178.3 2.5 %collective-permute-start.14 = (bf16[2,144,512]{2,1,0:T(8,128)(2,1)}, bf16[2,144,512]{2,1,0:T(8,128)(2,1)S(1)}, u32[]{:S(2)}, u32[]{:S(2)}) collective-permute-start(bf16[2,144,512]{2,1,0:T(8,128)(2,1)} %get-tuple-element.127), channel_id=1, source_target_pairs={{0,3},{1,2},{2,1},{3,0},{4,7},{5,6},{6,5},{7,4},{8,11},{9,10},{10,... | collective-permute-start | bytes 884744 | tf_op jit(solution)/shard_map/ppermute | solution.py:627
  180.8 3.6 %collective-permute-done.19.refs_3_ = bf16[2,144,512]{2,1,0:T(8,128)(2,1)S(1)} collective-permute-done((bf16[2,144,512]{2,1,0:T(8,128)(2,1)}, bf16[2,144,512]{2,1,0:T(8,128)(2,1)S(1)}, u32[]{:S(2)}, u32[]{:S(2)}) %collective-permute-start.19) | collective-permute-done | bytes 294944 | tf_op jit(solution)/shard_map/ppermute | solution.py:627
  184.4 0.7 copy-done.15
  185.1 3.9 %assemble_0_0.1 = (f32[16,128,512]{2,1,0:T(8,128)}, f32[8,2,128]{2,1,0:T(2,128)}) custom-call(s32[2]{0:T(128)} %pad_add_fusion.sc, f32[2,136,512]{2,1,0:T(8,128)} %get-tuple-element.132.refs_0_, bf16[2,144,512]{2,1,0:T(8,128)(2,1)} %copy-done.13, bf16[2,144,512]{2,1,0:T(8,128)(2,1)} %copy-done.14, bf16[2,144,512]{2,1,0:T(8,128)(2,1)} %copy-done.15), custom_call_target="tpu_custom_call" | custom-call | flops 1000000 | bytes 4194304 | tf_op jit(solution)/shard_map/assemble_0_0/pallas_call | solution.py:563
  189.0 0.7 copy-done.16
  189.7 2.8 %assemble_1_0.1 = (f32[16,128,512]{2,1,0:T(8,128)}, f32[8,2,128]{2,1,0:T(2,128)}) custom-call(s32[2]{0:T(128)} %pad_add_fusion.sc, f32[2,136,512]{2,1,0:T(8,128)} %get-tuple-element.129.refs_0_, bf16[2,144,512]{2,1,0:T(8,128)(2,1)} %copy-done.16, f32[16,128,512]{2,1,0:T(8,128)} %get-tuple-element.136.refs_2_, ...), custom_call_target="tpu_custom_call", output_to_operand_aliasing={{0}: (3, {}), {1}: (4, {})} | custom-call | flops 1000000 | bytes 2097152 | tf_op jit(solution)/shard_map/assemble_1_0/pallas_call | solution.py:563
  192.6 0.7 copy-done.12
  193.3 2.5 %assemble_1_2.1 = (f32[16,128,512]{2,1,0:T(8,128)}, f32[8,2,128]{2,1,0:T(2,128)}) custom-call(s32[2]{0:T(128)} %pad_add_fusion.sc, bf16[2,144,512]{2,1,0:T(8,128)(2,1)} %copy-done.12, f32[16,128,512]{2,1,0:T(8,128)} %get-tuple-element.138.refs_1_, f32[8,2,128]{2,1,0:T(2,128)} %get-tuple-element.139.refs_2_), custom_call_target="tpu_custom_call", output_to_operand_aliasing={{0}: (2, {}), {1}: (3, {})} | custom-call | flops 1000000 | bytes 1048576 | tf_op jit(solution)/shard_map/assemble_1_2/pallas_call | solution.py:563
  195.7 0.9 collective-permute-done.14.refs_0_
  196.6 0.7 copy-done.11
  197.3 2.5 %assemble_1_3.1 = (f32[16,128,512]{2,1,0:T(8,128)}, f32[8,2,128]{2,1,0:T(2,128)}) custom-call(s32[2]{0:T(128)} %pad_add_fusion.sc, bf16[2,144,512]{2,1,0:T(8,128)(2,1)} %copy-done.11, f32[16,128,512]{2,1,0:T(8,128)} %get-tuple-element.140.refs_1_, f32[8,2,128]{2,1,0:T(2,128)} %get-tuple-element.141.refs_2_), custom_call_target="tpu_custom_call", output_to_operand_aliasing={{0}: (2, {}), {1}: (3, {})} | custom-call | flops 1000000 | bytes 1048576 | tf_op jit(solution)/shard_map/assemble_1_3/pallas_call | solution.py:563
  (37 shorter events, 0.1 us)
Async XLA Ops:
  0.6 62.5 %copy-start = (s32[16,3072]{1,0:T(8,128)S(1)}, s32[16,3072]{1,0:T(8,128)}, u32[]{:S(2)}) copy-start(s32[16,3072]{1,0:T(8,128)} %param.7) | copy-start | bytes 589828
  6.4 39.3 %collective-permute-start = (bf16[528,1024]{1,0:T(8,128)(2,1)}, bf16[528,1024]{1,0:T(8,128)(2,1)S(1)}, u32[]{:S(2)}, u32[]{:S(2)}) collective-permute-start(bf16[528,1024]{1,0:T(8,128)(2,1)} %get-tuple-element.73), channel_id=1, source_target_pairs={{0,4},{4,8},{8,12},{12,16},{16,20},{20,24},{24,28},{28,32},{32,36}... | collective-permute-start | bytes 3244040 | tf_op jit(solution)/shard_map/ppermute | solution.py:634
  9.6 36.1 %collective-permute-start.1 = (bf16[528,1024]{1,0:T(8,128)(2,1)}, bf16[528,1024]{1,0:T(8,128)(2,1)S(1)}, u32[]{:S(2)}, u32[]{:S(2)}) collective-permute-start(bf16[528,1024]{1,0:T(8,128)(2,1)} %get-tuple-element.74), channel_id=1, source_target_pairs={{4,0},{8,4},{12,8},{16,12},{20,16},{24,20},{28,24},{32,28},{36,32}... | collective-permute-start | bytes 3244040 | tf_op jit(solution)/shard_map/ppermute | solution.py:635
  45.7 20.4 %copy-start.1 = (bf16[528,1024]{1,0:T(8,128)(2,1)}, bf16[528,1024]{1,0:T(8,128)(2,1)S(1)}, u32[]{:S(2)}) copy-start(bf16[528,1024]{1,0:T(8,128)(2,1)S(1)} %collective-permute-done.refs_0_.refs_1_.refs_2_.refs_3_.refs_4_) | copy-start | bytes 3244036
  45.7 20.4 %copy-start.2 = (bf16[528,1024]{1,0:T(8,128)(2,1)}, bf16[528,1024]{1,0:T(8,128)(2,1)S(1)}, u32[]{:S(2)}) copy-start(bf16[528,1024]{1,0:T(8,128)(2,1)S(1)} %collective-permute-done.1.refs_5_.refs_6_.refs_7_.refs_8_.refs_9_) | copy-start | bytes 3244036
  45.7 4.3 %collective-permute-start.4 = (bf16[26,128,128]{2,1,0:T(8,128)(2,1)}, bf16[26,128,128]{2,1,0:T(8,128)(2,1)S(1)}, u32[]{:S(2)}, u32[]{:S(2)}) collective-permute-start(bf16[26,128,128]{2,1,0:T(8,128)(2,1)} %get-tuple-element.82), channel_id=1, source_target_pairs={{0,1},{1,0},{2,3},{3,2},{4,5},{5,4},{6,7},{7,6},{8,9},{9,8},{10,11... | collective-permute-start | bytes 2555912 | tf_op jit(solution)/shard_map/ppermute | solution.py:627
  46.8 40.1 %collective-permute-start.2 = (bf16[26,128,128]{2,1,0:T(8,128)(2,1)}, bf16[26,128,128]{2,1,0:T(8,128)(2,1)}, u32[]{:S(2)}, u32[]{:S(2)}) collective-permute-start(bf16[26,128,128]{2,1,0:T(8,128)(2,1)} %get-tuple-element.79), channel_id=1, source_target_pairs={{0,2},{1,3},{2,0},{3,1},{4,6},{5,7},{6,4},{7,5},{8,10},{9,11},{10,... | collective-permute-start | bytes 2555912 | tf_op jit(solution)/shard_map/ppermute | solution.py:627
  48.9 39.1 %collective-permute-start.3 = (bf16[26,128,128]{2,1,0:T(8,128)(2,1)}, bf16[26,128,128]{2,1,0:T(8,128)(2,1)}, u32[]{:S(2)}, u32[]{:S(2)}) collective-permute-start(bf16[26,128,128]{2,1,0:T(8,128)(2,1)} %get-tuple-element.80), channel_id=1, source_target_pairs={{0,3},{1,2},{2,1},{3,0},{4,7},{5,6},{6,5},{7,4},{8,11},{9,10},{10,... | collective-permute-start | bytes 2555912 | tf_op jit(solution)/shard_map/ppermute | solution.py:627
  50.0 0.9 copy-start.3
  53.6 53.4 %collective-permute-start.5 = (bf16[2,13,128,128]{3,2,1,0:T(8,128)(2,1)}, bf16[2,13,128,128]{3,2,1,0:T(8,128)(2,1)S(1)}, u32[]{:S(2)}, u32[]{:S(2)}) collective-permute-start(bf16[2,13,128,128]{3,2,1,0:T(8,128)(2,1)} %get-tuple-element.99), channel_id=1, source_target_pairs={{0,4},{4,8},{8,12},{12,16},{16,20},{20,24},{24,28},{28,32},{32,36}... | collective-permute-start | bytes 2555912 | tf_op jit(solution)/shard_map/ppermute | solution.py:645
  55.5 51.5 %collective-permute-start.6 = (bf16[2,13,128,128]{3,2,1,0:T(8,128)(2,1)}, bf16[2,13,128,128]{3,2,1,0:T(8,128)(2,1)}, u32[]{:S(2)}, u32[]{:S(2)}) collective-permute-start(bf16[2,13,128,128]{3,2,1,0:T(8,128)(2,1)} %get-tuple-element.100), channel_id=1, source_target_pairs={{4,0},{8,4},{12,8},{16,12},{20,16},{24,20},{28,24},{32,28},{36,32}... | collective-permute-start | bytes 2555912 | tf_op jit(solution)/shard_map/ppermute | solution.py:646
  90.7 16.4 %copy-start.19 = (bf16[9,128,128]{2,1,0:T(8,128)(2,1)S(1)}, bf16[9,128,128]{2,1,0:T(8,128)(2,1)}, u32[]{:S(2)}) copy-start(bf16[9,128,128]{2,1,0:T(8,128)(2,1)} %get-tuple-element.117) | copy-start | bytes 884740
  90.7 17.3 %copy-start.18 = (bf16[9,128,128]{2,1,0:T(8,128)(2,1)S(1)}, bf16[9,128,128]{2,1,0:T(8,128)(2,1)}, u32[]{:S(2)}) copy-start(bf16[9,128,128]{2,1,0:T(8,128)(2,1)} %get-tuple-element.123) | copy-start | bytes 884740
  90.7 17.3 %copy-start.17 = (bf16[9,128,128]{2,1,0:T(8,128)(2,1)S(1)}, bf16[9,128,128]{2,1,0:T(8,128)(2,1)}, u32[]{:S(2)}) copy-start(bf16[9,128,128]{2,1,0:T(8,128)(2,1)} %get-tuple-element.124) | copy-start | bytes 884740
  107.0 37.2 %copy-start.9 = (bf16[2,13,128,128]{3,2,1,0:T(8,128)(2,1)}, bf16[2,13,128,128]{3,2,1,0:T(8,128)(2,1)S(1)}, u32[]{:S(2)}) copy-start(bf16[2,13,128,128]{3,2,1,0:T(8,128)(2,1)S(1)} %collective-permute-done.5.refs_2_) | copy-start | bytes 2555908
  107.0 4.4 %collective-permute-start.7 = (bf16[9,128,128]{2,1,0:T(8,128)(2,1)S(1)}, bf16[9,128,128]{2,1,0:T(8,128)(2,1)S(1)}, u32[]{:S(2)}, u32[]{:S(2)}) collective-permute-start(bf16[9,128,128]{2,1,0:T(8,128)(2,1)S(1)} %copy-done.19), channel_id=1, source_target_pairs={{0,1},{1,0},{2,3},{3,2},{4,5},{5,4},{6,7},{7,6},{8,9},{9,8},{10,11... | collective-permute-start | bytes 884744 | tf_op jit(solution)/shard_map/ppermute | solution.py:627
  108.0 12.9 %collective-permute-start.10 = (bf16[9,128,128]{2,1,0:T(8,128)(2,1)S(1)}, bf16[9,128,128]{2,1,0:T(8,128)(2,1)S(1)}, u32[]{:S(2)}, u32[]{:S(2)}) collective-permute-start(bf16[9,128,128]{2,1,0:T(8,128)(2,1)S(1)} %copy-done.18), channel_id=1, source_target_pairs={{0,2},{1,3},{2,0},{3,1},{4,6},{5,7},{6,4},{7,5},{8,10},{9,11},{10,... | collective-permute-start | bytes 884744 | tf_op jit(solution)/shard_map/ppermute | solution.py:627
  108.0 17.2 %collective-permute-start.11 = (bf16[9,128,128]{2,1,0:T(8,128)(2,1)S(1)}, bf16[9,128,128]{2,1,0:T(8,128)(2,1)S(1)}, u32[]{:S(2)}, u32[]{:S(2)}) collective-permute-start(bf16[9,128,128]{2,1,0:T(8,128)(2,1)S(1)} %copy-done.17), channel_id=1, source_target_pairs={{0,3},{1,2},{2,1},{3,0},{4,7},{5,6},{6,5},{7,4},{8,11},{9,10},{10,... | collective-permute-start | bytes 884744 | tf_op jit(solution)/shard_map/ppermute | solution.py:627
  111.4 13.8 %copy-start.4 = (bf16[9,128,128]{2,1,0:T(8,128)(2,1)}, bf16[9,128,128]{2,1,0:T(8,128)(2,1)S(1)}, u32[]{:S(2)}) copy-start(bf16[9,128,128]{2,1,0:T(8,128)(2,1)S(1)} %collective-permute-done.7.refs_1_) | copy-start | bytes 884740
  111.4 32.8 %collective-permute-start.8 = (bf16[2,13,128,128]{3,2,1,0:T(8,128)(2,1)}, bf16[2,13,128,128]{3,2,1,0:T(8,128)(2,1)S(1)}, u32[]{:S(2)}, u32[]{:S(2)}) collective-permute-start(bf16[2,13,128,128]{3,2,1,0:T(8,128)(2,1)} %get-tuple-element.118), channel_id=1, source_target_pairs={{0,4},{4,8},{8,12},{12,16},{16,20},{20,24},{24,28},{28,32},{32,36}... | collective-permute-start | bytes 2555912 | tf_op jit(solution)/shard_map/ppermute | solution.py:667
  113.3 30.9 %collective-permute-start.9 = (bf16[2,13,128,128]{3,2,1,0:T(8,128)(2,1)}, bf16[2,13,128,128]{3,2,1,0:T(8,128)(2,1)}, u32[]{:S(2)}, u32[]{:S(2)}) collective-permute-start(bf16[2,13,128,128]{3,2,1,0:T(8,128)(2,1)} %get-tuple-element.119), channel_id=1, source_target_pairs={{4,0},{8,4},{12,8},{16,12},{20,16},{24,20},{28,24},{32,28},{36,32}... | collective-permute-start | bytes 2555912 | tf_op jit(solution)/shard_map/ppermute | solution.py:668
  120.9 4.3 %copy-start.5 = (bf16[9,128,128]{2,1,0:T(8,128)(2,1)}, bf16[9,128,128]{2,1,0:T(8,128)(2,1)S(1)}, u32[]{:S(2)}) copy-start(bf16[9,128,128]{2,1,0:T(8,128)(2,1)S(1)} %collective-permute-done.10.refs_2_) | copy-start | bytes 884740
  125.2 0.7 copy-start.6
  128.5 29.8 %collective-permute-start.12 = (bf16[4,5,128,128]{3,2,1,0:T(8,128)(2,1)}, bf16[4,5,128,128]{3,2,1,0:T(8,128)(2,1)S(1)}, u32[]{:S(2)}, u32[]{:S(2)}) collective-permute-start(bf16[4,5,128,128]{3,2,1,0:T(8,128)(2,1)} %get-tuple-element.125), channel_id=1, source_target_pairs={{0,4},{4,8},{8,12},{12,16},{16,20},{20,24},{24,28},{28,32},{32,36}... | collective-permute-start | bytes 1966088 | tf_op jit(solution)/shard_map/ppermute | solution.py:670
  130.4 27.8 %collective-permute-start.13 = (bf16[4,5,128,128]{3,2,1,0:T(8,128)(2,1)}, bf16[4,5,128,128]{3,2,1,0:T(8,128)(2,1)S(1)}, u32[]{:S(2)}, u32[]{:S(2)}) collective-permute-start(bf16[4,5,128,128]{3,2,1,0:T(8,128)(2,1)} %get-tuple-element.126), channel_id=1, source_target_pairs={{4,0},{8,4},{12,8},{16,12},{20,16},{24,20},{28,24},{32,28},{36,32}... | collective-permute-start | bytes 1966088 | tf_op jit(solution)/shard_map/ppermute | solution.py:671
  144.2 0.9 copy-start.10
  158.3 0.8 copy-start.7
  158.3 1.1 copy-start.8
  166.0 12.3 %collective-permute-start.17 = (bf16[2,144,512]{2,1,0:T(8,128)(2,1)}, bf16[2,144,512]{2,1,0:T(8,128)(2,1)S(1)}, u32[]{:S(2)}, u32[]{:S(2)}) collective-permute-start(bf16[2,144,512]{2,1,0:T(8,128)(2,1)} %get-tuple-element.133), channel_id=1, source_target_pairs={{0,1},{1,0},{2,3},{3,2},{4,5},{5,4},{6,7},{7,6},{8,9},{9,8},{10,11... | collective-permute-start | bytes 884744 | tf_op jit(solution)/shard_map/ppermute | solution.py:627
  167.2 13.7 %collective-permute-start.18 = (bf16[2,144,512]{2,1,0:T(8,128)(2,1)}, bf16[2,144,512]{2,1,0:T(8,128)(2,1)S(1)}, u32[]{:S(2)}, u32[]{:S(2)}) collective-permute-start(bf16[2,144,512]{2,1,0:T(8,128)(2,1)} %get-tuple-element.134), channel_id=1, source_target_pairs={{0,2},{1,3},{2,0},{3,1},{4,6},{5,7},{6,4},{7,5},{8,10},{9,11},{10,... | collective-permute-start | bytes 884744 | tf_op jit(solution)/shard_map/ppermute | solution.py:627
  168.1 16.3 %collective-permute-start.19 = (bf16[2,144,512]{2,1,0:T(8,128)(2,1)}, bf16[2,144,512]{2,1,0:T(8,128)(2,1)S(1)}, u32[]{:S(2)}, u32[]{:S(2)}) collective-permute-start(bf16[2,144,512]{2,1,0:T(8,128)(2,1)} %get-tuple-element.135), channel_id=1, source_target_pairs={{0,3},{1,2},{2,1},{3,0},{4,7},{5,6},{6,5},{7,4},{8,11},{9,10},{10,... | collective-permute-start | bytes 884744 | tf_op jit(solution)/shard_map/ppermute | solution.py:627
  177.1 11.9 %collective-permute-start.16 = (bf16[2,144,512]{2,1,0:T(8,128)(2,1)}, bf16[2,144,512]{2,1,0:T(8,128)(2,1)S(1)}, u32[]{:S(2)}, u32[]{:S(2)}) collective-permute-start(bf16[2,144,512]{2,1,0:T(8,128)(2,1)} %get-tuple-element.130), channel_id=1, source_target_pairs={{0,1},{1,0},{2,3},{3,2},{4,5},{5,4},{6,7},{7,6},{8,9},{9,8},{10,11... | collective-permute-start | bytes 884744 | tf_op jit(solution)/shard_map/ppermute | solution.py:627
  177.3 15.3 %collective-permute-start.15 = (bf16[2,144,512]{2,1,0:T(8,128)(2,1)}, bf16[2,144,512]{2,1,0:T(8,128)(2,1)S(1)}, u32[]{:S(2)}, u32[]{:S(2)}) collective-permute-start(bf16[2,144,512]{2,1,0:T(8,128)(2,1)} %get-tuple-element.128), channel_id=1, source_target_pairs={{0,2},{1,3},{2,0},{3,1},{4,6},{5,7},{6,4},{7,5},{8,10},{9,11},{10,... | collective-permute-start | bytes 884744 | tf_op jit(solution)/shard_map/ppermute | solution.py:627
  178.3 6.2 %copy-start.13 = (bf16[2,144,512]{2,1,0:T(8,128)(2,1)}, bf16[2,144,512]{2,1,0:T(8,128)(2,1)S(1)}, u32[]{:S(2)}) copy-start(bf16[2,144,512]{2,1,0:T(8,128)(2,1)S(1)} %collective-permute-done.17.refs_1_) | copy-start | bytes 884740
  178.3 18.3 %collective-permute-start.14 = (bf16[2,144,512]{2,1,0:T(8,128)(2,1)}, bf16[2,144,512]{2,1,0:T(8,128)(2,1)S(1)}, u32[]{:S(2)}, u32[]{:S(2)}) collective-permute-start(bf16[2,144,512]{2,1,0:T(8,128)(2,1)} %get-tuple-element.127), channel_id=1, source_target_pairs={{0,3},{1,2},{2,1},{3,0},{4,7},{5,6},{6,5},{7,4},{8,11},{9,10},{10,... | collective-permute-start | bytes 884744 | tf_op jit(solution)/shard_map/ppermute | solution.py:627
  180.8 3.6 %copy-start.14 = (bf16[2,144,512]{2,1,0:T(8,128)(2,1)}, bf16[2,144,512]{2,1,0:T(8,128)(2,1)S(1)}, u32[]{:S(2)}) copy-start(bf16[2,144,512]{2,1,0:T(8,128)(2,1)S(1)} %collective-permute-done.18.refs_2_) | copy-start | bytes 884740
  184.4 0.7 copy-start.15
  189.0 0.7 copy-start.16
  192.6 0.7 copy-start.12
  196.6 0.7 copy-start.11

commit v2 on v1

--- a/solution.py
+++ b/solution.py
@@ -350,18 +350,18 @@
 
 
 def inner_plan():
-    return [
-        [(2 * t, 12, t, t) for t in range(6)],
-        [(INNER + 2 * t, INNER + 12, t, 26 + t) for t in range(6)],
-    ]
+    low = [(2 * t, 12, t, t) for t in range(6)]
+    high = [(INNER + 2 * t, INNER + 12, t, 26 + t) for t in range(6)]
+    at = 2 * INNER
+    outer = [(at + 2 * t, at + 4, t, 8 + t) for t in range(2)]
+    outer += [(at + 5 + 2 * t, at + 4, 2 + t, 22 + t) for t in range(2)]
+    return [low, high, outer]
 
 
 def outer_plan():
-    rows = [(2 * t, 4, t, 8 + t) for t in range(2)]
-    rows += [(5 + 2 * t, 4, 2 + t, 22 + t) for t in range(2)]
-    halo = [(10 + 2 * t, 9, 2 + t, 6 + t) for t in range(2)]
-    halo += [(14 + 2 * t, 18, t, 24 + t) for t in range(2)]
-    return [rows, halo]
+    rows = [(1 + 2 * t, 0, 2 + t, 6 + t) for t in range(2)]
+    rows += [(OUTER + 2 * t, OUTER + 4, t, 24 + t) for t in range(2)]
+    return [rows]
 
 
 def gram_rows(plan, patches, spread, pull, cells, scaled, mean_of, total):
@@ -454,13 +454,15 @@
 
 
 def inner_kernel(sc, spread, pull, *refs):
-    before, near, far, totals = refs[0:2], refs[2:4], refs[4:6], refs[6:8]
-    cells, scaled, mean_of, total, sems = refs[8:]
+    before, near, far, outer, totals = refs[0:2], refs[2:4], refs[4:6], refs[6:10], refs[10:12]
+    cells, scaled, mean_of, total, sems = refs[12:]
     me = sc[0]
     moves = []
     for side in range(2):
         for s in range(GROUPS):
             moves.append(((near, far)[s // 2][side].at[s % 2], side * INNER, INNER, me ^ s))
+    for s in range(GROUPS):
+        moves.append((outer[s], 2 * INNER, 9, me ^ s))
     fetch_all(moves, cells, sems)
     for i in range(OWN_PATCHES):
         total[i] = before[i // PAIR][i % PAIR]
@@ -469,9 +471,10 @@
         totals[i // PAIR][i % PAIR] = total[i]
 
 
-def running_gram(kernel, name, scalars, spread, pull, before, pieces):
+def running_gram(kernel, plan, name, scalars, spread, pull, before, pieces):
     vmem = pl.BlockSpec(memory_space=pltpu.VMEM)
     anywhere = pl.BlockSpec(memory_space=pl.ANY)
+    blocks = 2 * INNER + 9 * (len(plan) - 2)
     return pl.pallas_call(
         kernel,
         in_specs=[pl.BlockSpec(memory_space=pltpu.SMEM)]
@@ -480,11 +483,11 @@
         out_specs=[vmem] * 2,
         out_shape=[jax.ShapeDtypeStruct((PAIR, MEMBERS + 16, MEMBERS), F32)] * 2,
         scratch_shapes=[
-            pltpu.VMEM((2 * INNER, GROUPS, MINE, LANES), BF),
-            pltpu.VMEM((2, OWN_PATCHES, MEMBERS + 16, 6 * LANES), BF),
-            pltpu.VMEM((2 * INNER, 8, LANES), F32),
+            pltpu.VMEM((blocks, GROUPS, MINE, LANES), BF),
+            pltpu.VMEM((len(plan), OWN_PATCHES, MEMBERS + 16, 6 * LANES), BF),
+            pltpu.VMEM((blocks, 8, LANES), F32),
             pltpu.VMEM((OWN_PATCHES, MEMBERS + 16, MEMBERS), F32),
-            pltpu.SemaphoreType.DMA((8,)),
+            pltpu.SemaphoreType.DMA((12,)),
         ],
         compiler_params=pltpu.CompilerParams(vmem_limit_bytes=VMEM),
         cost_estimate=pl.CostEstimate(flops=10**7, bytes_accessed=35 * 2**20, transcendentals=0),
@@ -492,54 +495,53 @@
     )(scalars, spread, pull, *before, *pieces)
 
 
-def last_kernel(patches, sc, spread, pull, before, *refs):
-    own, low, high, outs = refs[0:4], refs[4], refs[5], refs[6:10]
-    cells, scaled, mean_of, total, sems = refs[10:]
+def last_kernel(patches, sc, spread, pull, before, low, high, *refs):
+    outs = refs[0:4]
+    cells, scaled, mean_of, total, sems = refs[4:]
     me = sc[0]
     moves = []
     for s in range(GROUPS):
-        moves.append((own[s].at[pl.ds(0, 9)], 0, 9, me ^ s))
-        moves.append((low.at[s], 9, OUTER, me ^ s))
-        moves.append((high.at[s], 14, OUTER, me ^ s))
+        moves.append((low.at[s], 0, OUTER, me ^ s))
+        moves.append((high.at[s], OUTER, OUTER, me ^ s))
     fetch_all(moves, cells, sems)
     total[...] = before[...]
     gram_rows(outer_plan(), patches, spread, pull, cells, scaled, mean_of, total)
-    for i in range(PAIR):
-        for s in range(GROUPS):
-            at = pl.multiple_of((me ^ s) * MINE, MINE)
+    for s in range(GROUPS):
+        at = pl.multiple_of((me ^ s) * MINE, MINE)
+        extra = []
+        for i in range(PAIR):
             projected = total[i, MEMBERS : MEMBERS + 8, pl.ds(at, MINE)]
             top = projected.astype(BF).astype(F32)
-            zero = jnp.zeros_like(top)
-            extra = jnp.concatenate([top, projected - top, zero, zero], axis=1)
+            extra += [top, projected - top]
             block = total[i, pl.ds(at, MINE), :]
-            if s == 0:
-                outs[s][i, 0:MINE, :] = block
-                outs[s][i, MINE : MINE + 8, :] = extra
-            else:
-                outs[s][i, 0:MINE, :] = block.astype(BF)
-                outs[s][i, MINE : MINE + 16, :] = jnp.concatenate([extra, extra], axis=0).astype(BF)
-
-
-def last_gram(patches, scalars, spread, pull, before, own, low, high):
+            outs[s][i * MINE : (i + 1) * MINE, :] = block.astype(outs[s].dtype)
+        extra = jnp.concatenate(extra, axis=1)
+        if s > 0:
+            extra = jnp.concatenate([extra, extra], axis=0).astype(BF)
+        outs[s][PAIR * MINE :, :] = extra
+
+
+def last_gram(patches, scalars, spread, pull, before, low, high):
     vmem = pl.BlockSpec(memory_space=pltpu.VMEM)
     anywhere = pl.BlockSpec(memory_space=pl.ANY)
+    rows = PAIR * MINE
     return pl.pallas_call(
         functools.partial(last_kernel, patches),
-        in_specs=[pl.BlockSpec(memory_space=pltpu.SMEM), vmem, vmem, vmem] + [anywhere] * 6,
+        in_specs=[pl.BlockSpec(memory_space=pltpu.SMEM), vmem, vmem, vmem] + [anywhere] * 2,
         out_specs=[vmem] * GROUPS,
-        out_shape=[jax.ShapeDtypeStruct((PAIR, MINE + 8, MEMBERS), F32)]
-        + [jax.ShapeDtypeStruct((PAIR, MINE + 16, MEMBERS), BF)] * (GROUPS - 1),
+        out_shape=[jax.ShapeDtypeStruct((rows + 8, MEMBERS), F32)]
+        + [jax.ShapeDtypeStruct((rows + 16, MEMBERS), BF)] * (GROUPS - 1),
         scratch_shapes=[
-            pltpu.VMEM((19, GROUPS, MINE, LANES), BF),
-            pltpu.VMEM((2, PAIR, MEMBERS + 16, 4 * LANES), BF),
-            pltpu.VMEM((19, 8, LANES), F32),
+            pltpu.VMEM((2 * OUTER, GROUPS, MINE, LANES), BF),
+            pltpu.VMEM((1, PAIR, MEMBERS + 16, 4 * LANES), BF),
+            pltpu.VMEM((2 * OUTER, 8, LANES), F32),
             pltpu.VMEM((PAIR, MEMBERS + 16, MEMBERS), F32),
-            pltpu.SemaphoreType.DMA((12,)),
+            pltpu.SemaphoreType.DMA((8,)),
         ],
         compiler_params=pltpu.CompilerParams(vmem_limit_bytes=VMEM),
-        cost_estimate=pl.CostEstimate(flops=10**7, bytes_accessed=30 * 2**20, transcendentals=0),
+        cost_estimate=pl.CostEstimate(flops=10**7, bytes_accessed=20 * 2**20, transcendentals=0),
         name=f"gram_last_{patches[0]}",
-    )(scalars, spread, pull, before, *own, low, high)
+    )(scalars, spread, pull, before, low, high)
 
 
 def assemble_kernel(which, sc, *refs):
@@ -549,9 +551,10 @@
         @pl.when(pl.program_id(0) == n)
         def _(n=n, s=s):
             for p in range(PAIR):
-                gram[p] = refs[n][p, 0:MINE, :].astype(F32)
-                extra = refs[n][p, MINE : MINE + (8 if s == 0 else 16), :].astype(F32)
-                proj[0, p : p + 1, :] = extra[0:1, 0:MINE] + extra[0:1, MINE : 2 * MINE]
+                gram[p] = refs[n][p * MINE : (p + 1) * MINE, :].astype(F32)
+                at = p * 2 * MINE
+                extra = refs[n][PAIR * MINE :, at : at + 2 * MINE].astype(F32)
+                proj[0, p : p + 1, :] = extra[0:1, 0:MINE] + extra[0:1, MINE:]
 
 
 def assemble(half, which, scalars, parts, begun):
@@ -565,7 +568,7 @@
         grid_spec=pltpu.PrefetchScalarGridSpec(
             num_scalar_prefetch=1,
             grid=(count,),
-            in_specs=[pl.BlockSpec(parts[s].shape, lambda n, sc: (0, 0, 0)) for s in which]
+            in_specs=[pl.BlockSpec(parts[s].shape, lambda n, sc: (0, 0)) for s in which]
             + [pl.BlockSpec(memory_space=pl.ANY)] * len(begun),
             out_specs=[
                 pl.BlockSpec((PAIR, MINE, MEMBERS), at),
@@ -655,7 +658,7 @@
     far_inner[0], far_inner[1], spread, pull, *outer = after(*far_inner, spread, pull, *outer)
     far_up, far_down = bundle("bundle_far", far_inner, INNER, INNER, 0)
     totals = running_gram(
-        own_kernel, "gram_own", scalars, spread, pull, [], near_inner + far_inner
+        own_kernel, own_plan(), "gram_own", scalars, spread, pull, [], near_inner + far_inner
     )
     near_low, near_high, far_up, far_down, *rest = after(
         near_low, near_high, far_up, far_down, *totals, *outer
@@ -670,15 +673,15 @@
     outer_low = lax.ppermute(outer_up, "grid", forward)
     outer_high = lax.ppermute(outer_down, "grid", backward)
 
-    halos = [near_low, near_high, far_low, far_high]
+    halos = [near_low, near_high, far_low, far_high, *outer]
     totals = running_gram(
-        inner_kernel, "gram_inner", scalars, spread, pull, totals, halos
+        inner_kernel, inner_plan(), "gram_inner", scalars, spread, pull, totals, halos
     )
     result = None
     for n in range(2):
         patches = [PAIR * n, PAIR * n + 1]
         sent = last_gram(
-            patches, scalars, spread, pull, totals[n], outer, outer_low, outer_high
+            patches, scalars, spread, pull, totals[n], outer_low, outer_high
         )
         parts = exchange(sent)
         for which in ([0, 1, 2, 3],) if n == 0 else ([0, 1], [2], [3]):

time: 201 us -> 198 us (0.985)
    pallas_call x2, Pallas kernels: 13.3 us -> 11 us  [last_gram(): pl.pallas_call(functools.partial(last_kernel, patches), in_specs=[pl.Bloc...]
    pallas_call x2, Pallas kernels: 21.2 us -> 23.5 us  [running_gram(): pl.pallas_call(kernel, in_specs=[pl.BlockSpec(memory_space=pltpu.SMEM)] +...]
  transfers between devices with their start and end apart: 20 -> 20, of which waited for: 7 -> 7; matrix products, arithmetic and copies ran while one was open for 2% -> 2% of each run, Pallas kernels for 47% -> 48%
where the time goes in v2:
time: 198 us; the launch traced here: 197 us
  Pallas kernels  109 us (55%)
  starting transfers between devices  55.5 us (28%)
  waiting for transfers between devices  22.8 us (12%)
  local copies, waits for them, and re-layouts  8.63 us (4%)
    pallas_call x2, Pallas kernels, observe(): pl.pallas_call(functools.partial(observe_kernel, inner), grid_spec=pltpu....  45.1 us
    pallas_call x2, Pallas kernels, running_gram(): pl.pallas_call(kernel, in_specs=[pl.BlockSpec(memory_space=pltpu.SMEM)] +...  23.5 us
    ppermute x12, starting transfers between devices, swap(): return lax.ppermute(x, 'mem', [(i, i ^ s) for i in range(GROUPS)])  17 us
    pallas_call x4, Pallas kernels, assemble(): pl.pallas_call(functools.partial(assemble_kernel, which), grid_spec=pltpu...  11.6 us
    pallas_call x2, Pallas kernels, last_gram(): pl.pallas_call(functools.partial(last_kernel, patches), in_specs=[pl.Bloc...  11 us
    ppermute x12, waiting for transfers between devices, swap(): return lax.ppermute(x, 'mem', [(i, i ^ s) for i in range(GROUPS)])  9.61 us
    pallas_call x3, Pallas kernels, bundle(): pl.pallas_call(functools.partial(bundle_kernel, plan, count, n), in_specs...  7.78 us
    ppermute x1, starting transfers between devices, per_device(): near_high = lax.ppermute(near_down, 'grid', backward)  7.58 us
  transfers between devices with their start and end apart: 20, of which 7 were waited for; matrix products, arithmetic and copies ran while one was open for 2% of the time, Pallas kernels for 48%

profile of v2, /device:TPU:3, one launch (start us, length us, event | category | flops | bytes accessed | tf_op | source)
XLA Modules:
  0.0 197.4 jit_solution(16608598079466543347)
XLA Ops:
  0.6 0.0 copy-start
  0.6 5.8 %edges.1 = (bf16[528,1024]{1,0:T(8,128)(2,1)}, bf16[528,1024]{1,0:T(8,128)(2,1)}) custom-call(bf16[2,2,16,1024]{3,2,1,0:T(8,128)(2,1)} %wind.5, bf16[128,2,16,1024]{3,2,1,0:T(8,128)(2,1)} %field.5), custom_call_target="tpu_custom_call" | custom-call | flops 10000000 | bytes 10485760 | tf_op jit(solution)/shard_map/edges/pallas_call | solution.py:74
  6.4 3.2 %collective-permute-start = (bf16[528,1024]{1,0:T(8,128)(2,1)}, bf16[528,1024]{1,0:T(8,128)(2,1)S(1)}, u32[]{:S(2)}, u32[]{:S(2)}) collective-permute-start(bf16[528,1024]{1,0:T(8,128)(2,1)} %get-tuple-element.73), channel_id=1, source_target_pairs={{0,4},{4,8},{8,12},{12,16},{16,20},{20,24},{24,28},{28,32},{32,36}... | collective-permute-start | bytes 3244040 | tf_op jit(solution)/shard_map/ppermute | solution.py:637
  9.6 6.8 %collective-permute-start.1 = (bf16[528,1024]{1,0:T(8,128)(2,1)}, bf16[528,1024]{1,0:T(8,128)(2,1)S(1)}, u32[]{:S(2)}, u32[]{:S(2)}) collective-permute-start(bf16[528,1024]{1,0:T(8,128)(2,1)} %get-tuple-element.74), channel_id=1, source_target_pairs={{4,0},{8,4},{12,8},{16,12},{20,16},{24,20},{28,24},{32,28},{36,32}... | collective-permute-start | bytes 3244040 | tf_op jit(solution)/shard_map/ppermute | solution.py:638
  16.4 0.6 pad_add_fusion.sc
  17.1 28.6 %observe_inner.1 = (bf16[26,128,128]{2,1,0:T(8,128)(2,1)}, bf16[26,128,128]{2,1,0:T(8,128)(2,1)}, bf16[26,128,128]{2,1,0:T(8,128)(2,1)}, bf16[26,128,128]{2,1,0:T(8,128)(2,1)}) custom-call(s32[2]{0:T(128)} %pad_add_fusion.sc, bf16[2,2,16,1024]{3,2,1,0:T(8,128)(2,1)} %wind.5, bf16[128,2,16,1024]{3,2,1,0:T(8,128)(2,1)} %field.5), custom_call_target="tpu_custom_call" | custom-call | flops 10000000 | bytes 73400320 | tf_op jit(solution)/shard_map/observe_inner/pallas_call | solution.py:256
  45.7 0.0 collective-permute-done.refs_0_.refs_1_.refs_2_.refs_3_.refs_4_
  45.7 0.0 collective-permute-done.1.refs_5_.refs_6_.refs_7_.refs_8_.refs_9_
  45.7 0.0 copy-start.2
  45.7 1.0 collective-permute-start.4
  46.7 2.2 %collective-permute-start.2 = (bf16[26,128,128]{2,1,0:T(8,128)(2,1)}, bf16[26,128,128]{2,1,0:T(8,128)(2,1)}, u32[]{:S(2)}, u32[]{:S(2)}) collective-permute-start(bf16[26,128,128]{2,1,0:T(8,128)(2,1)} %get-tuple-element.79), channel_id=1, source_target_pairs={{0,2},{1,3},{2,0},{3,1},{4,6},{5,7},{6,4},{7,5},{8,10},{9,11},{10,... | collective-permute-start | bytes 2555912 | tf_op jit(solution)/shard_map/ppermute | solution.py:630
  48.9 1.1 collective-permute-start.3
  50.0 0.0 collective-permute-done.4.refs_1_
  50.0 1.0 copy-done.3
  50.9 2.7 %bundle_near.1 = (bf16[2,13,128,128]{3,2,1,0:T(8,128)(2,1)}, bf16[2,13,128,128]{3,2,1,0:T(8,128)(2,1)}) custom-call(bf16[26,128,128]{2,1,0:T(8,128)(2,1)} %get-tuple-element.81.refs_0_, bf16[26,128,128]{2,1,0:T(8,128)(2,1)} %copy-done.3), custom_call_target="tpu_custom_call" | custom-call | bytes 4194304 | tf_op jit(solution)/shard_map/bundle_near/pallas_call | solution.py:606
  53.6 1.9 collective-permute-start.5
  55.5 7.6 %collective-permute-start.6 = (bf16[2,13,128,128]{3,2,1,0:T(8,128)(2,1)}, bf16[2,13,128,128]{3,2,1,0:T(8,128)(2,1)}, u32[]{:S(2)}, u32[]{:S(2)}) collective-permute-start(bf16[2,13,128,128]{3,2,1,0:T(8,128)(2,1)} %get-tuple-element.100), channel_id=1, source_target_pairs={{4,0},{8,4},{12,8},{16,12},{20,16},{24,20},{28,24},{32,28},{36,32}... | collective-permute-start | bytes 2555912 | tf_op jit(solution)/shard_map/ppermute | solution.py:649
  63.2 0.6 reshape.16.index
  63.8 1.0 constant_dynamic-slice_fusion
  64.8 0.6 reshape.18.values
  65.4 0.6 reshape.17.precision
  66.1 16.5 %observe_outer.1 = (bf16[9,128,128]{2,1,0:T(8,128)(2,1)}, bf16[9,128,128]{2,1,0:T(8,128)(2,1)}, bf16[9,128,128]{2,1,0:T(8,128)(2,1)}, bf16[9,128,128]{2,1,0:T(8,128)(2,1)}) custom-call(s32[2]{0:T(128)} %pad_add_fusion.sc, bf16[2,2,16,1024]{3,2,1,0:T(8,128)(2,1)} %wind.5, bf16[128,2,16,1024]{3,2,1,0:T(8,128)(2,1)} %field.5, bf16[528,1024]{1,0:T(8,128)(2,1)} %copy-done.1, ...), custom_call_target="tpu_custom_call" | custom-call | flops 10000000 | bytes 31457280 | tf_op jit(solution)/shard_map/observe_outer/pallas_call | solution.py:256
  82.5 4.3 %weigh.1 = (f32[4,32,128]{2,1,0:T(8,128)}, f32[4,32,128]{2,1,0:T(8,128)}) custom-call(s32[2]{0:T(128)} %pad_add_fusion.sc, s32[4,1,3072]{2,1,0:T(1,128)} %reshape.16.index, f32[4,1,3072]{2,1,0:T(1,128)} %reshape.17.precision, f32[4,1,3072]{2,1,0:T(1,128)} %reshape.18.values), custom_call_target="tpu_custom_call" | custom-call | flops 1000000000 | bytes 262144 | tf_op jit(solution)/shard_map/weigh/pallas_call | solution.py:324
  86.9 0.0 collective-permute-done.2.refs_0_.refs_2_
  86.9 1.1 collective-permute-done.3.refs_1_.refs_3_
  88.0 2.6 %bundle_far.1 = (bf16[2,13,128,128]{3,2,1,0:T(8,128)(2,1)}, bf16[2,13,128,128]{3,2,1,0:T(8,128)(2,1)}) custom-call(bf16[26,128,128]{2,1,0:T(8,128)(2,1)} %collective-permute-done.2.refs_0_.refs_2_, bf16[26,128,128]{2,1,0:T(8,128)(2,1)} %collective-permute-done.3.refs_1_.refs_3_), custom_call_target="tpu_custom_call" | custom-call | bytes 4194304 | tf_op jit(solution)/shard_map/bundle_far/pallas_call | solution.py:606
  90.6 10.0 %gram_own.1 = (f32[2,528,512]{2,1,0:T(8,128)}, f32[2,528,512]{2,1,0:T(8,128)}) custom-call(s32[2]{0:T(128)} %pad_add_fusion.sc, f32[4,32,128]{2,1,0:T(8,128)} %get-tuple-element.97.spread, f32[4,32,128]{2,1,0:T(8,128)} %get-tuple-element.98.pull, bf16[26,128,128]{2,1,0:T(8,128)(2,1)} %get-tuple-element.81.refs_0_, bf16[26,128,128]{2,1,0:T(8,128)(2,1)} %copy-done.3, ...), custom_call_target="tpu_custom_call" | custom-call | flops 10000000 | bytes 36700160 | tf_op jit(solution)/shard_map/gram_own/pallas_call | solution.py:478
  100.6 6.4 %collective-permute-done.5.refs_2_ = bf16[2,13,128,128]{3,2,1,0:T(8,128)(2,1)S(1)} collective-permute-done((bf16[2,13,128,128]{3,2,1,0:T(8,128)(2,1)}, bf16[2,13,128,128]{3,2,1,0:T(8,128)(2,1)S(1)}, u32[]{:S(2)}, u32[]{:S(2)}) %collective-permute-start.5) | collective-permute-done | bytes 852000 | tf_op jit(solution)/shard_map/ppermute | solution.py:648
  107.0 1.0 collective-permute-start.7
  108.0 0.0 collective-permute-start.10
  108.0 3.4 %collective-permute-start.11 = (bf16[9,128,128]{2,1,0:T(8,128)(2,1)S(1)}, bf16[9,128,128]{2,1,0:T(8,128)(2,1)S(1)}, u32[]{:S(2)}, u32[]{:S(2)}) collective-permute-start(bf16[9,128,128]{2,1,0:T(8,128)(2,1)S(1)} %copy-done.17), channel_id=1, source_target_pairs={{0,3},{1,2},{2,1},{3,0},{4,7},{5,6},{6,5},{7,4},{8,11},{9,10},{10,... | collective-permute-start | bytes 884744 | tf_op jit(solution)/shard_map/ppermute | solution.py:630
  111.4 0.0 collective-permute-done.7.refs_7_.refs_1_
  111.4 1.9 collective-permute-start.8
  113.3 7.6 %collective-permute-start.9 = (bf16[2,13,128,128]{3,2,1,0:T(8,128)(2,1)S(1)}, bf16[2,13,128,128]{3,2,1,0:T(8,128)(2,1)}, u32[]{:S(2)}, u32[]{:S(2)}) collective-permute-start(bf16[2,13,128,128]{3,2,1,0:T(8,128)(2,1)S(1)} %copy-done.16), channel_id=1, source_target_pairs={{4,0},{8,4},{12,8},{16,12},{20,16},{24,20},{28,24},{32,28},{36,32}... | collective-permute-start | bytes 2555912 | tf_op jit(solution)/shard_map/ppermute | solution.py:671
  120.9 4.3 %collective-permute-done.11.refs_9_.refs_3_ = bf16[9,128,128]{2,1,0:T(8,128)(2,1)S(1)} collective-permute-done((bf16[9,128,128]{2,1,0:T(8,128)(2,1)S(1)}, bf16[9,128,128]{2,1,0:T(8,128)(2,1)S(1)}, u32[]{:S(2)}, u32[]{:S(2)}) %collective-permute-start.11) | collective-permute-done | bytes 294944 | tf_op jit(solution)/shard_map/ppermute | solution.py:630
  125.2 0.7 copy-done.8
  125.9 2.5 %bundle_outer.1 = (bf16[4,5,128,128]{3,2,1,0:T(8,128)(2,1)}, bf16[4,5,128,128]{3,2,1,0:T(8,128)(2,1)}) custom-call(bf16[9,128,128]{2,1,0:T(8,128)(2,1)} %get-tuple-element.120.refs_6_.refs_0_, bf16[9,128,128]{2,1,0:T(8,128)(2,1)} %copy-done.6, bf16[9,128,128]{2,1,0:T(8,128)(2,1)} %copy-done.7, bf16[9,128,128]{2,1,0:T(8,128)(2,1)} %copy-done.8), custom_call_target="tpu_custom_call" | custom-call | bytes 4194304 | tf_op jit(solution)/shard_map/bundle_outer/pallas_call | solution.py:606
  128.5 1.9 collective-permute-start.12
  130.4 7.6 %collective-permute-start.13 = (bf16[4,5,128,128]{3,2,1,0:T(8,128)(2,1)}, bf16[4,5,128,128]{3,2,1,0:T(8,128)(2,1)S(1)}, u32[]{:S(2)}, u32[]{:S(2)}) collective-permute-start(bf16[4,5,128,128]{3,2,1,0:T(8,128)(2,1)} %get-tuple-element.126), channel_id=1, source_target_pairs={{4,0},{8,4},{12,8},{16,12},{20,16},{24,20},{28,24},{32,28},{36,32}... | collective-permute-start | bytes 1966088 | tf_op jit(solution)/shard_map/ppermute | solution.py:674
  138.0 6.3 %collective-permute-done.8.refs_4_ = bf16[2,13,128,128]{3,2,1,0:T(8,128)(2,1)} collective-permute-done((bf16[2,13,128,128]{3,2,1,0:T(8,128)(2,1)}, bf16[2,13,128,128]{3,2,1,0:T(8,128)(2,1)}, u32[]{:S(2)}, u32[]{:S(2)}) %collective-permute-start.8) | collective-permute-done | bytes 852000 | tf_op jit(solution)/shard_map/ppermute | solution.py:670
  144.3 13.5 %gram_inner.1 = (f32[2,528,512]{2,1,0:T(8,128)}, f32[2,528,512]{2,1,0:T(8,128)}) custom-call(s32[2]{0:T(128)} %pad_add_fusion.sc, f32[4,32,128]{2,1,0:T(8,128)} %get-tuple-element.97.spread, f32[4,32,128]{2,1,0:T(8,128)} %get-tuple-element.98.pull, f32[2,528,512]{2,1,0:T(8,128)} %get-tuple-element.111.refs_0_, f32[2,528,512]{2,1,0:T(8,128)} %get-tuple-element.112.refs_1_, ...), custom_call_target="tpu_custom_call" | custom-call | flops 10000000 | bytes 36700160 | tf_op jit(solution)/shard_map/gram_inner/pallas_call | solution.py:478
  157.8 0.4 collective-permute-done.12.low
  158.2 0.0 collective-permute-done.13.high
  158.2 0.8 copy-done.4
  159.1 0.2 copy-done.5
  159.3 5.5 %gram_last_0.1 = (f32[264,512]{1,0:T(8,128)}, bf16[272,512]{1,0:T(8,128)(2,1)}, bf16[272,512]{1,0:T(8,128)(2,1)}, bf16[272,512]{1,0:T(8,128)(2,1)}) custom-call(s32[2]{0:T(128)} %pad_add_fusion.sc, f32[4,32,128]{2,1,0:T(8,128)} %get-tuple-element.97.spread, f32[4,32,128]{2,1,0:T(8,128)} %get-tuple-element.98.pull, f32[2,528,512]{2,1,0:T(8,128)} %get-tuple-element.131.before, ...), custom_call_target="tpu_custom_call" | custom-call | flops 10000000 | bytes 20971520 | tf_op jit(solution)/shard_map/gram_last_0/pallas_call | solution.py:528
  164.8 1.4 collective-permute-start.17
  166.2 1.0 collective-permute-start.18
  167.2 2.3 %collective-permute-start.19 = (bf16[272,512]{1,0:T(8,128)(2,1)}, bf16[272,512]{1,0:T(8,128)(2,1)S(1)}, u32[]{:S(2)}, u32[]{:S(2)}) collective-permute-start(bf16[272,512]{1,0:T(8,128)(2,1)} %get-tuple-element.135), channel_id=1, source_target_pairs={{0,3},{1,2},{2,1},{3,0},{4,7},{5,6},{6,5},{7,4},{8,11},{9,10},{10,... | collective-permute-start | bytes 835592 | tf_op jit(solution)/shard_map/ppermute | solution.py:630
  169.5 5.5 %gram_last_2.1 = (f32[264,512]{1,0:T(8,128)}, bf16[272,512]{1,0:T(8,128)(2,1)}, bf16[272,512]{1,0:T(8,128)(2,1)}, bf16[272,512]{1,0:T(8,128)(2,1)}) custom-call(s32[2]{0:T(128)} %pad_add_fusion.sc, f32[4,32,128]{2,1,0:T(8,128)} %get-tuple-element.97.spread, f32[4,32,128]{2,1,0:T(8,128)} %get-tuple-element.98.pull, f32[2,528,512]{2,1,0:T(8,128)} %get-tuple-element.124.before, ...), custom_call_target="tpu_custom_call" | custom-call | flops 10000000 | bytes 20971520 | tf_op jit(solution)/shard_map/gram_last_2/pallas_call | solution.py:528
  175.0 0.2 collective-permute-start.16
  175.2 0.9 collective-permute-start.15
  176.1 0.0 collective-permute-done.17.refs_1_
  176.1 2.6 %collective-permute-start.14 = (bf16[272,512]{1,0:T(8,128)(2,1)}, bf16[272,512]{1,0:T(8,128)(2,1)S(1)}, u32[]{:S(2)}, u32[]{:S(2)}) collective-permute-start(bf16[272,512]{1,0:T(8,128)(2,1)} %get-tuple-element.127), channel_id=1, source_target_pairs={{0,3},{1,2},{2,1},{3,0},{4,7},{5,6},{6,5},{7,4},{8,11},{9,10},{10,... | collective-permute-start | bytes 835592 | tf_op jit(solution)/shard_map/ppermute | solution.py:630
  178.7 4.1 %collective-permute-done.19.refs_3_ = bf16[272,512]{1,0:T(8,128)(2,1)S(1)} collective-permute-done((bf16[272,512]{1,0:T(8,128)(2,1)}, bf16[272,512]{1,0:T(8,128)(2,1)S(1)}, u32[]{:S(2)}, u32[]{:S(2)}) %collective-permute-start.19) | collective-permute-done | bytes 278560 | tf_op jit(solution)/shard_map/ppermute | solution.py:630
  182.8 0.7 copy-done.14
  183.5 3.9 %assemble_0_0.1 = (f32[16,128,512]{2,1,0:T(8,128)}, f32[8,2,128]{2,1,0:T(2,128)}) custom-call(s32[2]{0:T(128)} %pad_add_fusion.sc, f32[264,512]{1,0:T(8,128)} %get-tuple-element.132.refs_0_, bf16[272,512]{1,0:T(8,128)(2,1)} %copy-done.11, bf16[272,512]{1,0:T(8,128)(2,1)} %copy-done.12, bf16[272,512]{1,0:T(8,128)(2,1)} %copy-done.14), custom_call_target="tpu_custom_call" | custom-call | flops 1000000 | bytes 4194304 | tf_op jit(solution)/shard_map/assemble_0_0/pallas_call | solution.py:566
  187.4 0.7 copy-done.15
  188.1 2.8 %assemble_1_0.1 = (f32[16,128,512]{2,1,0:T(8,128)}, f32[8,2,128]{2,1,0:T(2,128)}) custom-call(s32[2]{0:T(128)} %pad_add_fusion.sc, f32[264,512]{1,0:T(8,128)} %get-tuple-element.129.refs_0_, bf16[272,512]{1,0:T(8,128)(2,1)} %copy-done.15, f32[16,128,512]{2,1,0:T(8,128)} %get-tuple-element.136.refs_2_, ...), custom_call_target="tpu_custom_call", output_to_operand_aliasing={{0}: (3, {}), {1}: (4, {})} | custom-call | flops 1000000 | bytes 2097152 | tf_op jit(solution)/shard_map/assemble_1_0/pallas_call | solution.py:566
  191.0 0.7 copy-done.13
  191.7 2.4 %assemble_1_2.1 = (f32[16,128,512]{2,1,0:T(8,128)}, f32[8,2,128]{2,1,0:T(2,128)}) custom-call(s32[2]{0:T(128)} %pad_add_fusion.sc, bf16[272,512]{1,0:T(8,128)(2,1)} %copy-done.13, f32[16,128,512]{2,1,0:T(8,128)} %get-tuple-element.138.refs_1_, f32[8,2,128]{2,1,0:T(2,128)} %get-tuple-element.139.refs_2_), custom_call_target="tpu_custom_call", output_to_operand_aliasing={{0}: (2, {}), {1}: (3, {})} | custom-call | flops 1000000 | bytes 1048576 | tf_op jit(solution)/shard_map/assemble_1_2/pallas_call | solution.py:566
  194.1 0.1 collective-permute-done.14.refs_0_
  194.2 0.7 copy-done.10
  194.9 2.4 %assemble_1_3.1 = (f32[16,128,512]{2,1,0:T(8,128)}, f32[8,2,128]{2,1,0:T(2,128)}) custom-call(s32[2]{0:T(128)} %pad_add_fusion.sc, bf16[272,512]{1,0:T(8,128)(2,1)} %copy-done.10, f32[16,128,512]{2,1,0:T(8,128)} %get-tuple-element.140.refs_1_, f32[8,2,128]{2,1,0:T(2,128)} %get-tuple-element.141.refs_2_), custom_call_target="tpu_custom_call", output_to_operand_aliasing={{0}: (2, {}), {1}: (3, {})} | custom-call | flops 1000000 | bytes 1048576 | tf_op jit(solution)/shard_map/assemble_1_3/pallas_call | solution.py:566
  (37 shorter events, 0.1 us)
Async XLA Ops:
  0.6 62.5 %copy-start = (s32[16,3072]{1,0:T(8,128)S(1)}, s32[16,3072]{1,0:T(8,128)}, u32[]{:S(2)}) copy-start(s32[16,3072]{1,0:T(8,128)} %param.7) | copy-start | bytes 589828
  6.4 39.3 %collective-permute-start = (bf16[528,1024]{1,0:T(8,128)(2,1)}, bf16[528,1024]{1,0:T(8,128)(2,1)S(1)}, u32[]{:S(2)}, u32[]{:S(2)}) collective-permute-start(bf16[528,1024]{1,0:T(8,128)(2,1)} %get-tuple-element.73), channel_id=1, source_target_pairs={{0,4},{4,8},{8,12},{12,16},{16,20},{20,24},{24,28},{28,32},{32,36}... | collective-permute-start | bytes 3244040 | tf_op jit(solution)/shard_map/ppermute | solution.py:637
  9.6 36.1 %collective-permute-start.1 = (bf16[528,1024]{1,0:T(8,128)(2,1)}, bf16[528,1024]{1,0:T(8,128)(2,1)S(1)}, u32[]{:S(2)}, u32[]{:S(2)}) collective-permute-start(bf16[528,1024]{1,0:T(8,128)(2,1)} %get-tuple-element.74), channel_id=1, source_target_pairs={{4,0},{8,4},{12,8},{16,12},{20,16},{24,20},{28,24},{32,28},{36,32}... | collective-permute-start | bytes 3244040 | tf_op jit(solution)/shard_map/ppermute | solution.py:638
  45.7 20.4 %copy-start.1 = (bf16[528,1024]{1,0:T(8,128)(2,1)}, bf16[528,1024]{1,0:T(8,128)(2,1)S(1)}, u32[]{:S(2)}) copy-start(bf16[528,1024]{1,0:T(8,128)(2,1)S(1)} %collective-permute-done.refs_0_.refs_1_.refs_2_.refs_3_.refs_4_) | copy-start | bytes 3244036
  45.7 20.4 %copy-start.2 = (bf16[528,1024]{1,0:T(8,128)(2,1)}, bf16[528,1024]{1,0:T(8,128)(2,1)S(1)}, u32[]{:S(2)}) copy-start(bf16[528,1024]{1,0:T(8,128)(2,1)S(1)} %collective-permute-done.1.refs_5_.refs_6_.refs_7_.refs_8_.refs_9_) | copy-start | bytes 3244036
  45.7 4.3 %collective-permute-start.4 = (bf16[26,128,128]{2,1,0:T(8,128)(2,1)}, bf16[26,128,128]{2,1,0:T(8,128)(2,1)S(1)}, u32[]{:S(2)}, u32[]{:S(2)}) collective-permute-start(bf16[26,128,128]{2,1,0:T(8,128)(2,1)} %get-tuple-element.82), channel_id=1, source_target_pairs={{0,1},{1,0},{2,3},{3,2},{4,5},{5,4},{6,7},{7,6},{8,9},{9,8},{10,11... | collective-permute-start | bytes 2555912 | tf_op jit(solution)/shard_map/ppermute | solution.py:630
  46.7 40.1 %collective-permute-start.2 = (bf16[26,128,128]{2,1,0:T(8,128)(2,1)}, bf16[26,128,128]{2,1,0:T(8,128)(2,1)}, u32[]{:S(2)}, u32[]{:S(2)}) collective-permute-start(bf16[26,128,128]{2,1,0:T(8,128)(2,1)} %get-tuple-element.79), channel_id=1, source_target_pairs={{0,2},{1,3},{2,0},{3,1},{4,6},{5,7},{6,4},{7,5},{8,10},{9,11},{10,... | collective-permute-start | bytes 2555912 | tf_op jit(solution)/shard_map/ppermute | solution.py:630
  48.9 39.1 %collective-permute-start.3 = (bf16[26,128,128]{2,1,0:T(8,128)(2,1)}, bf16[26,128,128]{2,1,0:T(8,128)(2,1)}, u32[]{:S(2)}, u32[]{:S(2)}) collective-permute-start(bf16[26,128,128]{2,1,0:T(8,128)(2,1)} %get-tuple-element.80), channel_id=1, source_target_pairs={{0,3},{1,2},{2,1},{3,0},{4,7},{5,6},{6,5},{7,4},{8,11},{9,10},{10,... | collective-permute-start | bytes 2555912 | tf_op jit(solution)/shard_map/ppermute | solution.py:630
  50.0 1.0 copy-start.3
  53.6 53.4 %collective-permute-start.5 = (bf16[2,13,128,128]{3,2,1,0:T(8,128)(2,1)}, bf16[2,13,128,128]{3,2,1,0:T(8,128)(2,1)S(1)}, u32[]{:S(2)}, u32[]{:S(2)}) collective-permute-start(bf16[2,13,128,128]{3,2,1,0:T(8,128)(2,1)} %get-tuple-element.99), channel_id=1, source_target_pairs={{0,4},{4,8},{8,12},{12,16},{16,20},{20,24},{24,28},{28,32},{32,36}... | collective-permute-start | bytes 2555912 | tf_op jit(solution)/shard_map/ppermute | solution.py:648
  55.5 51.5 %collective-permute-start.6 = (bf16[2,13,128,128]{3,2,1,0:T(8,128)(2,1)}, bf16[2,13,128,128]{3,2,1,0:T(8,128)(2,1)}, u32[]{:S(2)}, u32[]{:S(2)}) collective-permute-start(bf16[2,13,128,128]{3,2,1,0:T(8,128)(2,1)} %get-tuple-element.100), channel_id=1, source_target_pairs={{4,0},{8,4},{12,8},{16,12},{20,16},{24,20},{28,24},{32,28},{36,32}... | collective-permute-start | bytes 2555912 | tf_op jit(solution)/shard_map/ppermute | solution.py:649
  90.6 16.4 %copy-start.19 = (bf16[9,128,128]{2,1,0:T(8,128)(2,1)S(1)}, bf16[9,128,128]{2,1,0:T(8,128)(2,1)}, u32[]{:S(2)}) copy-start(bf16[9,128,128]{2,1,0:T(8,128)(2,1)} %get-tuple-element.117) | copy-start | bytes 884740
  90.6 17.4 %copy-start.18 = (bf16[9,128,128]{2,1,0:T(8,128)(2,1)S(1)}, bf16[9,128,128]{2,1,0:T(8,128)(2,1)}, u32[]{:S(2)}) copy-start(bf16[9,128,128]{2,1,0:T(8,128)(2,1)} %get-tuple-element.122) | copy-start | bytes 884740
  90.6 17.4 %copy-start.17 = (bf16[9,128,128]{2,1,0:T(8,128)(2,1)S(1)}, bf16[9,128,128]{2,1,0:T(8,128)(2,1)}, u32[]{:S(2)}) copy-start(bf16[9,128,128]{2,1,0:T(8,128)(2,1)} %get-tuple-element.123) | copy-start | bytes 884740
  90.6 22.7 %copy-start.16 = (bf16[2,13,128,128]{3,2,1,0:T(8,128)(2,1)S(1)}, bf16[2,13,128,128]{3,2,1,0:T(8,128)(2,1)}, u32[]{:S(2)}) copy-start(bf16[2,13,128,128]{3,2,1,0:T(8,128)(2,1)} %get-tuple-element.119) | copy-start | bytes 2555908
  107.0 37.3 %copy-start.9 = (bf16[2,13,128,128]{3,2,1,0:T(8,128)(2,1)}, bf16[2,13,128,128]{3,2,1,0:T(8,128)(2,1)S(1)}, u32[]{:S(2)}) copy-start(bf16[2,13,128,128]{3,2,1,0:T(8,128)(2,1)S(1)} %collective-permute-done.5.refs_2_) | copy-start | bytes 2555908
  107.0 4.4 %collective-permute-start.7 = (bf16[9,128,128]{2,1,0:T(8,128)(2,1)S(1)}, bf16[9,128,128]{2,1,0:T(8,128)(2,1)S(1)}, u32[]{:S(2)}, u32[]{:S(2)}) collective-permute-start(bf16[9,128,128]{2,1,0:T(8,128)(2,1)S(1)} %copy-done.19), channel_id=1, source_target_pairs={{0,1},{1,0},{2,3},{3,2},{4,5},{5,4},{6,7},{7,6},{8,9},{9,8},{10,11... | collective-permute-start | bytes 884744 | tf_op jit(solution)/shard_map/ppermute | solution.py:630
  108.0 12.9 %collective-permute-start.10 = (bf16[9,128,128]{2,1,0:T(8,128)(2,1)S(1)}, bf16[9,128,128]{2,1,0:T(8,128)(2,1)S(1)}, u32[]{:S(2)}, u32[]{:S(2)}) collective-permute-start(bf16[9,128,128]{2,1,0:T(8,128)(2,1)S(1)} %copy-done.18), channel_id=1, source_target_pairs={{0,2},{1,3},{2,0},{3,1},{4,6},{5,7},{6,4},{7,5},{8,10},{9,11},{10,... | collective-permute-start | bytes 884744 | tf_op jit(solution)/shard_map/ppermute | solution.py:630
  108.0 17.2 %collective-permute-start.11 = (bf16[9,128,128]{2,1,0:T(8,128)(2,1)S(1)}, bf16[9,128,128]{2,1,0:T(8,128)(2,1)S(1)}, u32[]{:S(2)}, u32[]{:S(2)}) collective-permute-start(bf16[9,128,128]{2,1,0:T(8,128)(2,1)S(1)} %copy-done.17), channel_id=1, source_target_pairs={{0,3},{1,2},{2,1},{3,0},{4,7},{5,6},{6,5},{7,4},{8,11},{9,10},{10,... | collective-permute-start | bytes 884744 | tf_op jit(solution)/shard_map/ppermute | solution.py:630
  111.4 13.8 %copy-start.6 = (bf16[9,128,128]{2,1,0:T(8,128)(2,1)}, bf16[9,128,128]{2,1,0:T(8,128)(2,1)S(1)}, u32[]{:S(2)}) copy-start(bf16[9,128,128]{2,1,0:T(8,128)(2,1)S(1)} %collective-permute-done.7.refs_7_.refs_1_) | copy-start | bytes 884740
  111.4 32.9 %collective-permute-start.8 = (bf16[2,13,128,128]{3,2,1,0:T(8,128)(2,1)}, bf16[2,13,128,128]{3,2,1,0:T(8,128)(2,1)}, u32[]{:S(2)}, u32[]{:S(2)}) collective-permute-start(bf16[2,13,128,128]{3,2,1,0:T(8,128)(2,1)} %get-tuple-element.118), channel_id=1, source_target_pairs={{0,4},{4,8},{8,12},{12,16},{16,20},{20,24},{24,28},{28,32},{32,36}... | collective-permute-start | bytes 2555912 | tf_op jit(solution)/shard_map/ppermute | solution.py:670
  113.3 31.0 %collective-permute-start.9 = (bf16[2,13,128,128]{3,2,1,0:T(8,128)(2,1)S(1)}, bf16[2,13,128,128]{3,2,1,0:T(8,128)(2,1)}, u32[]{:S(2)}, u32[]{:S(2)}) collective-permute-start(bf16[2,13,128,128]{3,2,1,0:T(8,128)(2,1)S(1)} %copy-done.16), channel_id=1, source_target_pairs={{4,0},{8,4},{12,8},{16,12},{20,16},{24,20},{28,24},{32,28},{36,32}... | collective-permute-start | bytes 2555912 | tf_op jit(solution)/shard_map/ppermute | solution.py:671
  120.9 4.3 %copy-start.7 = (bf16[9,128,128]{2,1,0:T(8,128)(2,1)}, bf16[9,128,128]{2,1,0:T(8,128)(2,1)S(1)}, u32[]{:S(2)}) copy-start(bf16[9,128,128]{2,1,0:T(8,128)(2,1)S(1)} %collective-permute-done.10.refs_8_.refs_2_) | copy-start | bytes 884740
  125.2 0.7 copy-start.8
  128.5 29.8 %collective-permute-start.12 = (bf16[4,5,128,128]{3,2,1,0:T(8,128)(2,1)}, bf16[4,5,128,128]{3,2,1,0:T(8,128)(2,1)S(1)}, u32[]{:S(2)}, u32[]{:S(2)}) collective-permute-start(bf16[4,5,128,128]{3,2,1,0:T(8,128)(2,1)} %get-tuple-element.125), channel_id=1, source_target_pairs={{0,4},{4,8},{8,12},{12,16},{16,20},{20,24},{24,28},{28,32},{32,36}... | collective-permute-start | bytes 1966088 | tf_op jit(solution)/shard_map/ppermute | solution.py:673
  130.4 27.9 %collective-permute-start.13 = (bf16[4,5,128,128]{3,2,1,0:T(8,128)(2,1)}, bf16[4,5,128,128]{3,2,1,0:T(8,128)(2,1)S(1)}, u32[]{:S(2)}, u32[]{:S(2)}) collective-permute-start(bf16[4,5,128,128]{3,2,1,0:T(8,128)(2,1)} %get-tuple-element.126), channel_id=1, source_target_pairs={{4,0},{8,4},{12,8},{16,12},{20,16},{24,20},{28,24},{32,28},{36,32}... | collective-permute-start | bytes 1966088 | tf_op jit(solution)/shard_map/ppermute | solution.py:674
  158.2 0.8 copy-start.4
  158.2 1.1 copy-start.5
  164.8 11.3 %collective-permute-start.17 = (bf16[272,512]{1,0:T(8,128)(2,1)}, bf16[272,512]{1,0:T(8,128)(2,1)S(1)}, u32[]{:S(2)}, u32[]{:S(2)}) collective-permute-start(bf16[272,512]{1,0:T(8,128)(2,1)} %get-tuple-element.133), channel_id=1, source_target_pairs={{0,1},{1,0},{2,3},{3,2},{4,5},{5,4},{6,7},{7,6},{8,9},{9,8},{10,11... | collective-permute-start | bytes 835592 | tf_op jit(solution)/shard_map/ppermute | solution.py:630
  166.2 12.5 %collective-permute-start.18 = (bf16[272,512]{1,0:T(8,128)(2,1)}, bf16[272,512]{1,0:T(8,128)(2,1)S(1)}, u32[]{:S(2)}, u32[]{:S(2)}) collective-permute-start(bf16[272,512]{1,0:T(8,128)(2,1)} %get-tuple-element.134), channel_id=1, source_target_pairs={{0,2},{1,3},{2,0},{3,1},{4,6},{5,7},{6,4},{7,5},{8,10},{9,11},{10,... | collective-permute-start | bytes 835592 | tf_op jit(solution)/shard_map/ppermute | solution.py:630
  167.2 15.6 %collective-permute-start.19 = (bf16[272,512]{1,0:T(8,128)(2,1)}, bf16[272,512]{1,0:T(8,128)(2,1)S(1)}, u32[]{:S(2)}, u32[]{:S(2)}) collective-permute-start(bf16[272,512]{1,0:T(8,128)(2,1)} %get-tuple-element.135), channel_id=1, source_target_pairs={{0,3},{1,2},{2,1},{3,0},{4,7},{5,6},{6,5},{7,4},{8,11},{9,10},{10,... | collective-permute-start | bytes 835592 | tf_op jit(solution)/shard_map/ppermute | solution.py:630
  175.0 12.4 %collective-permute-start.16 = (bf16[272,512]{1,0:T(8,128)(2,1)}, bf16[272,512]{1,0:T(8,128)(2,1)S(1)}, u32[]{:S(2)}, u32[]{:S(2)}) collective-permute-start(bf16[272,512]{1,0:T(8,128)(2,1)} %get-tuple-element.130), channel_id=1, source_target_pairs={{0,1},{1,0},{2,3},{3,2},{4,5},{5,4},{6,7},{7,6},{8,9},{9,8},{10,11... | collective-permute-start | bytes 835592 | tf_op jit(solution)/shard_map/ppermute | solution.py:630
  175.2 15.8 %collective-permute-start.15 = (bf16[272,512]{1,0:T(8,128)(2,1)}, bf16[272,512]{1,0:T(8,128)(2,1)S(1)}, u32[]{:S(2)}, u32[]{:S(2)}) collective-permute-start(bf16[272,512]{1,0:T(8,128)(2,1)} %get-tuple-element.128), channel_id=1, source_target_pairs={{0,2},{1,3},{2,0},{3,1},{4,6},{5,7},{6,4},{7,5},{8,10},{9,11},{10,... | collective-permute-start | bytes 835592 | tf_op jit(solution)/shard_map/ppermute | solution.py:630
  176.1 6.6 %copy-start.11 = (bf16[272,512]{1,0:T(8,128)(2,1)}, bf16[272,512]{1,0:T(8,128)(2,1)S(1)}, u32[]{:S(2)}) copy-start(bf16[272,512]{1,0:T(8,128)(2,1)S(1)} %collective-permute-done.17.refs_1_) | copy-start | bytes 835588
  176.1 18.1 %collective-permute-start.14 = (bf16[272,512]{1,0:T(8,128)(2,1)}, bf16[272,512]{1,0:T(8,128)(2,1)S(1)}, u32[]{:S(2)}, u32[]{:S(2)}) collective-permute-start(bf16[272,512]{1,0:T(8,128)(2,1)} %get-tuple-element.127), channel_id=1, source_target_pairs={{0,3},{1,2},{2,1},{3,0},{4,7},{5,6},{6,5},{7,4},{8,11},{9,10},{10,... | collective-permute-start | bytes 835592 | tf_op jit(solution)/shard_map/ppermute | solution.py:630
  178.7 4.1 %copy-start.12 = (bf16[272,512]{1,0:T(8,128)(2,1)}, bf16[272,512]{1,0:T(8,128)(2,1)S(1)}, u32[]{:S(2)}) copy-start(bf16[272,512]{1,0:T(8,128)(2,1)S(1)} %collective-permute-done.18.refs_2_) | copy-start | bytes 835588
  182.8 0.7 copy-start.14
  187.4 0.7 copy-start.15
  191.0 0.7 copy-start.13
  194.2 0.7 copy-start.10

commit v3 on v2

--- a/solution.py
+++ b/solution.py
@@ -432,12 +432,13 @@
         multiply(*ready)
 
 
-def fetch_all(moves, cells, sems):
+def fetch_all(moves, cells, sems, meanwhile):
     copies = []
     for n, (src, at, count, group) in enumerate(moves):
         copy = pltpu.make_async_copy(src, cells.at[pl.ds(at, count), group], sems.at[n])
         copy.start()
         copies.append(copy)
+    meanwhile()
     for copy in copies:
         copy.wait()
 
@@ -446,8 +447,11 @@
     pieces, totals = refs[0:4], refs[4:6]
     cells, scaled, mean_of, total, sems = refs[6:]
     me = sc[0]
-    fetch_all([(pieces[s], 0, 2 * INNER, me ^ s) for s in range(GROUPS)], cells, sems)
-    total[...] = jnp.zeros_like(total)
+
+    def clear():
+        total[...] = jnp.zeros_like(total)
+
+    fetch_all([(pieces[s], 0, 2 * INNER, me ^ s) for s in range(GROUPS)], cells, sems, clear)
     gram_rows(own_plan(), list(range(OWN_PATCHES)), spread, pull, cells, scaled, mean_of, total)
     for i in range(OWN_PATCHES):
         totals[i // PAIR][i % PAIR] = total[i]
@@ -463,9 +467,12 @@
             moves.append(((near, far)[s // 2][side].at[s % 2], side * INNER, INNER, me ^ s))
     for s in range(GROUPS):
         moves.append((outer[s], 2 * INNER, 9, me ^ s))
-    fetch_all(moves, cells, sems)
-    for i in range(OWN_PATCHES):
-        total[i] = before[i // PAIR][i % PAIR]
+
+    def begin():
+        for i in range(OWN_PATCHES):
+            total[i] = before[i // PAIR][i % PAIR]
+
+    fetch_all(moves, cells, sems, begin)
     gram_rows(inner_plan(), list(range(OWN_PATCHES)), spread, pull, cells, scaled, mean_of, total)
     for i in range(OWN_PATCHES):
         totals[i // PAIR][i % PAIR] = total[i]
@@ -503,8 +510,11 @@
     for s in range(GROUPS):
         moves.append((low.at[s], 0, OUTER, me ^ s))
         moves.append((high.at[s], OUTER, OUTER, me ^ s))
-    fetch_all(moves, cells, sems)
-    total[...] = before[...]
+
+    def begin():
+        total[...] = before[...]
+
+    fetch_all(moves, cells, sems, begin)
     gram_rows(outer_plan(), patches, spread, pull, cells, scaled, mean_of, total)
     for s in range(GROUPS):
         at = pl.multiple_of((me ^ s) * MINE, MINE)

time: 198 us -> 198 us (level)
  no operation moved by 1% of the time
where the time goes in v3:
time: 198 us; the launch traced here: 197 us
  Pallas kernels  109 us (55%)
  starting transfers between devices  55.5 us (28%)
  waiting for transfers between devices  22.8 us (12%)
  local copies, waits for them, and re-layouts  8.63 us (4%)
    pallas_call x2, Pallas kernels, observe(): pl.pallas_call(functools.partial(observe_kernel, inner), grid_spec=pltpu....  45.1 us
    pallas_call x2, Pallas kernels, running_gram(): pl.pallas_call(kernel, in_specs=[pl.BlockSpec(memory_space=pltpu.SMEM)] +...  23.5 us
    ppermute x12, starting transfers between devices, swap(): return lax.ppermute(x, 'mem', [(i, i ^ s) for i in range(GROUPS)])  17 us
    pallas_call x4, Pallas kernels, assemble(): pl.pallas_call(functools.partial(assemble_kernel, which), grid_spec=pltpu...  11.6 us
    pallas_call x2, Pallas kernels, last_gram(): pl.pallas_call(functools.partial(last_kernel, patches), in_specs=[pl.Bloc...  11 us
    ppermute x12, waiting for transfers between devices, swap(): return lax.ppermute(x, 'mem', [(i, i ^ s) for i in range(GROUPS)])  9.63 us
    pallas_call x3, Pallas kernels, bundle(): pl.pallas_call(functools.partial(bundle_kernel, plan, count, n), in_specs...  7.78 us
    ppermute x1, starting transfers between devices, per_device(): near_high = lax.ppermute(near_down, 'grid', backward)  7.58 us
  transfers between devices with their start and end apart: 20, of which 7 were waited for; matrix products, arithmetic and copies ran while one was open for 2% of the time, Pallas kernels for 48%

profile of v3, /device:TPU:3, one launch (start us, length us, event | category | flops | bytes accessed | tf_op | source)
XLA Modules:
  0.0 197.4 jit_solution(12435860680584726847)
XLA Ops:
  0.6 0.0 copy-start
  0.6 5.8 %edges.1 = (bf16[528,1024]{1,0:T(8,128)(2,1)}, bf16[528,1024]{1,0:T(8,128)(2,1)}) custom-call(bf16[2,2,16,1024]{3,2,1,0:T(8,128)(2,1)} %wind.5, bf16[128,2,16,1024]{3,2,1,0:T(8,128)(2,1)} %field.5), custom_call_target="tpu_custom_call" | custom-call | flops 10000000 | bytes 10485760 | tf_op jit(solution)/shard_map/edges/pallas_call | solution.py:74
  6.4 3.2 %collective-permute-start = (bf16[528,1024]{1,0:T(8,128)(2,1)}, bf16[528,1024]{1,0:T(8,128)(2,1)S(1)}, u32[]{:S(2)}, u32[]{:S(2)}) collective-permute-start(bf16[528,1024]{1,0:T(8,128)(2,1)} %get-tuple-element.73), channel_id=1, source_target_pairs={{0,4},{4,8},{8,12},{12,16},{16,20},{20,24},{24,28},{28,32},{32,36}... | collective-permute-start | bytes 3244040 | tf_op jit(solution)/shard_map/ppermute | solution.py:647
  9.6 6.8 %collective-permute-start.1 = (bf16[528,1024]{1,0:T(8,128)(2,1)}, bf16[528,1024]{1,0:T(8,128)(2,1)S(1)}, u32[]{:S(2)}, u32[]{:S(2)}) collective-permute-start(bf16[528,1024]{1,0:T(8,128)(2,1)} %get-tuple-element.74), channel_id=1, source_target_pairs={{4,0},{8,4},{12,8},{16,12},{20,16},{24,20},{28,24},{32,28},{36,32}... | collective-permute-start | bytes 3244040 | tf_op jit(solution)/shard_map/ppermute | solution.py:648
  16.4 0.6 pad_add_fusion.sc
  17.1 28.6 %observe_inner.1 = (bf16[26,128,128]{2,1,0:T(8,128)(2,1)}, bf16[26,128,128]{2,1,0:T(8,128)(2,1)}, bf16[26,128,128]{2,1,0:T(8,128)(2,1)}, bf16[26,128,128]{2,1,0:T(8,128)(2,1)}) custom-call(s32[2]{0:T(128)} %pad_add_fusion.sc, bf16[2,2,16,1024]{3,2,1,0:T(8,128)(2,1)} %wind.5, bf16[128,2,16,1024]{3,2,1,0:T(8,128)(2,1)} %field.5), custom_call_target="tpu_custom_call" | custom-call | flops 10000000 | bytes 73400320 | tf_op jit(solution)/shard_map/observe_inner/pallas_call | solution.py:256
  45.7 0.0 collective-permute-done.refs_0_.refs_1_.refs_2_.refs_3_.refs_4_
  45.7 0.0 collective-permute-done.1.refs_5_.refs_6_.refs_7_.refs_8_.refs_9_
  45.7 0.0 copy-start.2
  45.7 1.0 collective-permute-start.4
  46.7 2.2 %collective-permute-start.2 = (bf16[26,128,128]{2,1,0:T(8,128)(2,1)}, bf16[26,128,128]{2,1,0:T(8,128)(2,1)}, u32[]{:S(2)}, u32[]{:S(2)}) collective-permute-start(bf16[26,128,128]{2,1,0:T(8,128)(2,1)} %get-tuple-element.79), channel_id=1, source_target_pairs={{0,2},{1,3},{2,0},{3,1},{4,6},{5,7},{6,4},{7,5},{8,10},{9,11},{10,... | collective-permute-start | bytes 2555912 | tf_op jit(solution)/shard_map/ppermute | solution.py:640
  48.9 1.1 collective-permute-start.3
  50.0 0.0 collective-permute-done.4.refs_1_
  50.0 1.0 copy-done.3
  50.9 2.7 %bundle_near.1 = (bf16[2,13,128,128]{3,2,1,0:T(8,128)(2,1)}, bf16[2,13,128,128]{3,2,1,0:T(8,128)(2,1)}) custom-call(bf16[26,128,128]{2,1,0:T(8,128)(2,1)} %get-tuple-element.81.refs_0_, bf16[26,128,128]{2,1,0:T(8,128)(2,1)} %copy-done.3), custom_call_target="tpu_custom_call" | custom-call | bytes 4194304 | tf_op jit(solution)/shard_map/bundle_near/pallas_call | solution.py:616
  53.6 1.9 collective-permute-start.5
  55.5 7.6 %collective-permute-start.6 = (bf16[2,13,128,128]{3,2,1,0:T(8,128)(2,1)}, bf16[2,13,128,128]{3,2,1,0:T(8,128)(2,1)}, u32[]{:S(2)}, u32[]{:S(2)}) collective-permute-start(bf16[2,13,128,128]{3,2,1,0:T(8,128)(2,1)} %get-tuple-element.100), channel_id=1, source_target_pairs={{4,0},{8,4},{12,8},{16,12},{20,16},{24,20},{28,24},{32,28},{36,32}... | collective-permute-start | bytes 2555912 | tf_op jit(solution)/shard_map/ppermute | solution.py:659
  63.2 0.6 reshape.16.index
  63.8 1.0 constant_dynamic-slice_fusion
  64.8 0.6 reshape.18.values
  65.4 0.6 reshape.17.precision
  66.1 16.5 %observe_outer.1 = (bf16[9,128,128]{2,1,0:T(8,128)(2,1)}, bf16[9,128,128]{2,1,0:T(8,128)(2,1)}, bf16[9,128,128]{2,1,0:T(8,128)(2,1)}, bf16[9,128,128]{2,1,0:T(8,128)(2,1)}) custom-call(s32[2]{0:T(128)} %pad_add_fusion.sc, bf16[2,2,16,1024]{3,2,1,0:T(8,128)(2,1)} %wind.5, bf16[128,2,16,1024]{3,2,1,0:T(8,128)(2,1)} %field.5, bf16[528,1024]{1,0:T(8,128)(2,1)} %copy-done.1, ...), custom_call_target="tpu_custom_call" | custom-call | flops 10000000 | bytes 31457280 | tf_op jit(solution)/shard_map/observe_outer/pallas_call | solution.py:256
  82.5 4.3 %weigh.1 = (f32[4,32,128]{2,1,0:T(8,128)}, f32[4,32,128]{2,1,0:T(8,128)}) custom-call(s32[2]{0:T(128)} %pad_add_fusion.sc, s32[4,1,3072]{2,1,0:T(1,128)} %reshape.16.index, f32[4,1,3072]{2,1,0:T(1,128)} %reshape.17.precision, f32[4,1,3072]{2,1,0:T(1,128)} %reshape.18.values), custom_call_target="tpu_custom_call" | custom-call | flops 1000000000 | bytes 262144 | tf_op jit(solution)/shard_map/weigh/pallas_call | solution.py:324
  86.9 0.0 collective-permute-done.2.refs_0_.refs_2_
  86.9 1.1 collective-permute-done.3.refs_1_.refs_3_
  88.0 2.6 %bundle_far.1 = (bf16[2,13,128,128]{3,2,1,0:T(8,128)(2,1)}, bf16[2,13,128,128]{3,2,1,0:T(8,128)(2,1)}) custom-call(bf16[26,128,128]{2,1,0:T(8,128)(2,1)} %collective-permute-done.2.refs_0_.refs_2_, bf16[26,128,128]{2,1,0:T(8,128)(2,1)} %collective-permute-done.3.refs_1_.refs_3_), custom_call_target="tpu_custom_call" | custom-call | bytes 4194304 | tf_op jit(solution)/shard_map/bundle_far/pallas_call | solution.py:616
  90.6 10.0 %gram_own.1 = (f32[2,528,512]{2,1,0:T(8,128)}, f32[2,528,512]{2,1,0:T(8,128)}) custom-call(s32[2]{0:T(128)} %pad_add_fusion.sc, f32[4,32,128]{2,1,0:T(8,128)} %get-tuple-element.97.spread, f32[4,32,128]{2,1,0:T(8,128)} %get-tuple-element.98.pull, bf16[26,128,128]{2,1,0:T(8,128)(2,1)} %get-tuple-element.81.refs_0_, bf16[26,128,128]{2,1,0:T(8,128)(2,1)} %copy-done.3, ...), custom_call_target="tpu_custom_call" | custom-call | flops 10000000 | bytes 36700160 | tf_op jit(solution)/shard_map/gram_own/pallas_call | solution.py:485
  100.6 6.4 %collective-permute-done.5.refs_2_ = bf16[2,13,128,128]{3,2,1,0:T(8,128)(2,1)S(1)} collective-permute-done((bf16[2,13,128,128]{3,2,1,0:T(8,128)(2,1)}, bf16[2,13,128,128]{3,2,1,0:T(8,128)(2,1)S(1)}, u32[]{:S(2)}, u32[]{:S(2)}) %collective-permute-start.5) | collective-permute-done | bytes 852000 | tf_op jit(solution)/shard_map/ppermute | solution.py:658
  107.0 1.0 collective-permute-start.7
  108.0 0.0 collective-permute-start.10
  108.0 3.4 %collective-permute-start.11 = (bf16[9,128,128]{2,1,0:T(8,128)(2,1)S(1)}, bf16[9,128,128]{2,1,0:T(8,128)(2,1)S(1)}, u32[]{:S(2)}, u32[]{:S(2)}) collective-permute-start(bf16[9,128,128]{2,1,0:T(8,128)(2,1)S(1)} %copy-done.17), channel_id=1, source_target_pairs={{0,3},{1,2},{2,1},{3,0},{4,7},{5,6},{6,5},{7,4},{8,11},{9,10},{10,... | collective-permute-start | bytes 884744 | tf_op jit(solution)/shard_map/ppermute | solution.py:640
  111.4 0.0 collective-permute-done.7.refs_7_.refs_1_
  111.4 1.9 collective-permute-start.8
  113.3 7.6 %collective-permute-start.9 = (bf16[2,13,128,128]{3,2,1,0:T(8,128)(2,1)S(1)}, bf16[2,13,128,128]{3,2,1,0:T(8,128)(2,1)}, u32[]{:S(2)}, u32[]{:S(2)}) collective-permute-start(bf16[2,13,128,128]{3,2,1,0:T(8,128)(2,1)S(1)} %copy-done.16), channel_id=1, source_target_pairs={{4,0},{8,4},{12,8},{16,12},{20,16},{24,20},{28,24},{32,28},{36,32}... | collective-permute-start | bytes 2555912 | tf_op jit(solution)/shard_map/ppermute | solution.py:681
  120.9 4.3 %collective-permute-done.11.refs_9_.refs_3_ = bf16[9,128,128]{2,1,0:T(8,128)(2,1)S(1)} collective-permute-done((bf16[9,128,128]{2,1,0:T(8,128)(2,1)S(1)}, bf16[9,128,128]{2,1,0:T(8,128)(2,1)S(1)}, u32[]{:S(2)}, u32[]{:S(2)}) %collective-permute-start.11) | collective-permute-done | bytes 294944 | tf_op jit(solution)/shard_map/ppermute | solution.py:640
  125.2 0.7 copy-done.8
  125.9 2.5 %bundle_outer.1 = (bf16[4,5,128,128]{3,2,1,0:T(8,128)(2,1)}, bf16[4,5,128,128]{3,2,1,0:T(8,128)(2,1)}) custom-call(bf16[9,128,128]{2,1,0:T(8,128)(2,1)} %get-tuple-element.120.refs_6_.refs_0_, bf16[9,128,128]{2,1,0:T(8,128)(2,1)} %copy-done.6, bf16[9,128,128]{2,1,0:T(8,128)(2,1)} %copy-done.7, bf16[9,128,128]{2,1,0:T(8,128)(2,1)} %copy-done.8), custom_call_target="tpu_custom_call" | custom-call | bytes 4194304 | tf_op jit(solution)/shard_map/bundle_outer/pallas_call | solution.py:616
  128.5 1.9 collective-permute-start.12
  130.4 7.6 %collective-permute-start.13 = (bf16[4,5,128,128]{3,2,1,0:T(8,128)(2,1)}, bf16[4,5,128,128]{3,2,1,0:T(8,128)(2,1)S(1)}, u32[]{:S(2)}, u32[]{:S(2)}) collective-permute-start(bf16[4,5,128,128]{3,2,1,0:T(8,128)(2,1)} %get-tuple-element.126), channel_id=1, source_target_pairs={{4,0},{8,4},{12,8},{16,12},{20,16},{24,20},{28,24},{32,28},{36,32}... | collective-permute-start | bytes 1966088 | tf_op jit(solution)/shard_map/ppermute | solution.py:684
  138.0 6.3 %collective-permute-done.8.refs_4_ = bf16[2,13,128,128]{3,2,1,0:T(8,128)(2,1)} collective-permute-done((bf16[2,13,128,128]{3,2,1,0:T(8,128)(2,1)}, bf16[2,13,128,128]{3,2,1,0:T(8,128)(2,1)}, u32[]{:S(2)}, u32[]{:S(2)}) %collective-permute-start.8) | collective-permute-done | bytes 852000 | tf_op jit(solution)/shard_map/ppermute | solution.py:680
  144.3 13.5 %gram_inner.1 = (f32[2,528,512]{2,1,0:T(8,128)}, f32[2,528,512]{2,1,0:T(8,128)}) custom-call(s32[2]{0:T(128)} %pad_add_fusion.sc, f32[4,32,128]{2,1,0:T(8,128)} %get-tuple-element.97.spread, f32[4,32,128]{2,1,0:T(8,128)} %get-tuple-element.98.pull, f32[2,528,512]{2,1,0:T(8,128)} %get-tuple-element.111.refs_0_, f32[2,528,512]{2,1,0:T(8,128)} %get-tuple-element.112.refs_1_, ...), custom_call_target="tpu_custom_call" | custom-call | flops 10000000 | bytes 36700160 | tf_op jit(solution)/shard_map/gram_inner/pallas_call | solution.py:485
  157.8 0.4 collective-permute-done.12.low
  158.2 0.0 collective-permute-done.13.high
  158.2 0.8 copy-done.4
  159.1 0.2 copy-done.5
  159.3 5.5 %gram_last_0.1 = (f32[264,512]{1,0:T(8,128)}, bf16[272,512]{1,0:T(8,128)(2,1)}, bf16[272,512]{1,0:T(8,128)(2,1)}, bf16[272,512]{1,0:T(8,128)(2,1)}) custom-call(s32[2]{0:T(128)} %pad_add_fusion.sc, f32[4,32,128]{2,1,0:T(8,128)} %get-tuple-element.97.spread, f32[4,32,128]{2,1,0:T(8,128)} %get-tuple-element.98.pull, f32[2,528,512]{2,1,0:T(8,128)} %get-tuple-element.131.before, ...), custom_call_target="tpu_custom_call" | custom-call | flops 10000000 | bytes 20971520 | tf_op jit(solution)/shard_map/gram_last_0/pallas_call | solution.py:538
  164.8 1.4 collective-permute-start.17
  166.2 1.0 collective-permute-start.18
  167.2 2.3 %collective-permute-start.19 = (bf16[272,512]{1,0:T(8,128)(2,1)}, bf16[272,512]{1,0:T(8,128)(2,1)S(1)}, u32[]{:S(2)}, u32[]{:S(2)}) collective-permute-start(bf16[272,512]{1,0:T(8,128)(2,1)} %get-tuple-element.135), channel_id=1, source_target_pairs={{0,3},{1,2},{2,1},{3,0},{4,7},{5,6},{6,5},{7,4},{8,11},{9,10},{10,... | collective-permute-start | bytes 835592 | tf_op jit(solution)/shard_map/ppermute | solution.py:640
  169.5 5.5 %gram_last_2.1 = (f32[264,512]{1,0:T(8,128)}, bf16[272,512]{1,0:T(8,128)(2,1)}, bf16[272,512]{1,0:T(8,128)(2,1)}, bf16[272,512]{1,0:T(8,128)(2,1)}) custom-call(s32[2]{0:T(128)} %pad_add_fusion.sc, f32[4,32,128]{2,1,0:T(8,128)} %get-tuple-element.97.spread, f32[4,32,128]{2,1,0:T(8,128)} %get-tuple-element.98.pull, f32[2,528,512]{2,1,0:T(8,128)} %get-tuple-element.124.before, ...), custom_call_target="tpu_custom_call" | custom-call | flops 10000000 | bytes 20971520 | tf_op jit(solution)/shard_map/gram_last_2/pallas_call | solution.py:538
  175.0 0.2 collective-permute-start.16
  175.2 0.9 collective-permute-start.15
  176.1 2.6 %collective-permute-start.14 = (bf16[272,512]{1,0:T(8,128)(2,1)}, bf16[272,512]{1,0:T(8,128)(2,1)S(1)}, u32[]{:S(2)}, u32[]{:S(2)}) collective-permute-start(bf16[272,512]{1,0:T(8,128)(2,1)} %get-tuple-element.127), channel_id=1, source_target_pairs={{0,3},{1,2},{2,1},{3,0},{4,7},{5,6},{6,5},{7,4},{8,11},{9,10},{10,... | collective-permute-start | bytes 835592 | tf_op jit(solution)/shard_map/ppermute | solution.py:640
  178.7 0.0 collective-permute-done.18.refs_2_
  178.7 4.1 %collective-permute-done.19.refs_3_ = bf16[272,512]{1,0:T(8,128)(2,1)S(1)} collective-permute-done((bf16[272,512]{1,0:T(8,128)(2,1)}, bf16[272,512]{1,0:T(8,128)(2,1)S(1)}, u32[]{:S(2)}, u32[]{:S(2)}) %collective-permute-start.19) | collective-permute-done | bytes 278560 | tf_op jit(solution)/shard_map/ppermute | solution.py:640
  182.8 0.7 copy-done.14
  183.5 3.9 %assemble_0_0.1 = (f32[16,128,512]{2,1,0:T(8,128)}, f32[8,2,128]{2,1,0:T(2,128)}) custom-call(s32[2]{0:T(128)} %pad_add_fusion.sc, f32[264,512]{1,0:T(8,128)} %get-tuple-element.132.refs_0_, bf16[272,512]{1,0:T(8,128)(2,1)} %copy-done.11, bf16[272,512]{1,0:T(8,128)(2,1)} %copy-done.12, bf16[272,512]{1,0:T(8,128)(2,1)} %copy-done.14), custom_call_target="tpu_custom_call" | custom-call | flops 1000000 | bytes 4194304 | tf_op jit(solution)/shard_map/assemble_0_0/pallas_call | solution.py:576
  187.4 0.7 copy-done.15
  188.1 2.8 %assemble_1_0.1 = (f32[16,128,512]{2,1,0:T(8,128)}, f32[8,2,128]{2,1,0:T(2,128)}) custom-call(s32[2]{0:T(128)} %pad_add_fusion.sc, f32[264,512]{1,0:T(8,128)} %get-tuple-element.129.refs_0_, bf16[272,512]{1,0:T(8,128)(2,1)} %copy-done.15, f32[16,128,512]{2,1,0:T(8,128)} %get-tuple-element.136.refs_2_, ...), custom_call_target="tpu_custom_call", output_to_operand_aliasing={{0}: (3, {}), {1}: (4, {})} | custom-call | flops 1000000 | bytes 2097152 | tf_op jit(solution)/shard_map/assemble_1_0/pallas_call | solution.py:576
  191.0 0.7 copy-done.13
  191.7 2.4 %assemble_1_2.1 = (f32[16,128,512]{2,1,0:T(8,128)}, f32[8,2,128]{2,1,0:T(2,128)}) custom-call(s32[2]{0:T(128)} %pad_add_fusion.sc, bf16[272,512]{1,0:T(8,128)(2,1)} %copy-done.13, f32[16,128,512]{2,1,0:T(8,128)} %get-tuple-element.138.refs_1_, f32[8,2,128]{2,1,0:T(2,128)} %get-tuple-element.139.refs_2_), custom_call_target="tpu_custom_call", output_to_operand_aliasing={{0}: (2, {}), {1}: (3, {})} | custom-call | flops 1000000 | bytes 1048576 | tf_op jit(solution)/shard_map/assemble_1_2/pallas_call | solution.py:576
  194.1 0.1 collective-permute-done.14.refs_0_
  194.3 0.7 copy-done.10
  195.0 2.4 %assemble_1_3.1 = (f32[16,128,512]{2,1,0:T(8,128)}, f32[8,2,128]{2,1,0:T(2,128)}) custom-call(s32[2]{0:T(128)} %pad_add_fusion.sc, bf16[272,512]{1,0:T(8,128)(2,1)} %copy-done.10, f32[16,128,512]{2,1,0:T(8,128)} %get-tuple-element.140.refs_1_, f32[8,2,128]{2,1,0:T(2,128)} %get-tuple-element.141.refs_2_), custom_call_target="tpu_custom_call", output_to_operand_aliasing={{0}: (2, {}), {1}: (3, {})} | custom-call | flops 1000000 | bytes 1048576 | tf_op jit(solution)/shard_map/assemble_1_3/pallas_call | solution.py:576
  (37 shorter events, 0.1 us)
Async XLA Ops:
  0.6 62.5 %copy-start = (s32[16,3072]{1,0:T(8,128)S(1)}, s32[16,3072]{1,0:T(8,128)}, u32[]{:S(2)}) copy-start(s32[16,3072]{1,0:T(8,128)} %param.7) | copy-start | bytes 589828
  6.4 39.3 %collective-permute-start = (bf16[528,1024]{1,0:T(8,128)(2,1)}, bf16[528,1024]{1,0:T(8,128)(2,1)S(1)}, u32[]{:S(2)}, u32[]{:S(2)}) collective-permute-start(bf16[528,1024]{1,0:T(8,128)(2,1)} %get-tuple-element.73), channel_id=1, source_target_pairs={{0,4},{4,8},{8,12},{12,16},{16,20},{20,24},{24,28},{28,32},{32,36}... | collective-permute-start | bytes 3244040 | tf_op jit(solution)/shard_map/ppermute | solution.py:647
  9.6 36.1 %collective-permute-start.1 = (bf16[528,1024]{1,0:T(8,128)(2,1)}, bf16[528,1024]{1,0:T(8,128)(2,1)S(1)}, u32[]{:S(2)}, u32[]{:S(2)}) collective-permute-start(bf16[528,1024]{1,0:T(8,128)(2,1)} %get-tuple-element.74), channel_id=1, source_target_pairs={{4,0},{8,4},{12,8},{16,12},{20,16},{24,20},{28,24},{32,28},{36,32}... | collective-permute-start | bytes 3244040 | tf_op jit(solution)/shard_map/ppermute | solution.py:648
  45.7 20.4 %copy-start.1 = (bf16[528,1024]{1,0:T(8,128)(2,1)}, bf16[528,1024]{1,0:T(8,128)(2,1)S(1)}, u32[]{:S(2)}) copy-start(bf16[528,1024]{1,0:T(8,128)(2,1)S(1)} %collective-permute-done.refs_0_.refs_1_.refs_2_.refs_3_.refs_4_) | copy-start | bytes 3244036
  45.7 20.4 %copy-start.2 = (bf16[528,1024]{1,0:T(8,128)(2,1)}, bf16[528,1024]{1,0:T(8,128)(2,1)S(1)}, u32[]{:S(2)}) copy-start(bf16[528,1024]{1,0:T(8,128)(2,1)S(1)} %collective-permute-done.1.refs_5_.refs_6_.refs_7_.refs_8_.refs_9_) | copy-start | bytes 3244036
  45.7 4.3 %collective-permute-start.4 = (bf16[26,128,128]{2,1,0:T(8,128)(2,1)}, bf16[26,128,128]{2,1,0:T(8,128)(2,1)S(1)}, u32[]{:S(2)}, u32[]{:S(2)}) collective-permute-start(bf16[26,128,128]{2,1,0:T(8,128)(2,1)} %get-tuple-element.82), channel_id=1, source_target_pairs={{0,1},{1,0},{2,3},{3,2},{4,5},{5,4},{6,7},{7,6},{8,9},{9,8},{10,11... | collective-permute-start | bytes 2555912 | tf_op jit(solution)/shard_map/ppermute | solution.py:640
  46.7 40.1 %collective-permute-start.2 = (bf16[26,128,128]{2,1,0:T(8,128)(2,1)}, bf16[26,128,128]{2,1,0:T(8,128)(2,1)}, u32[]{:S(2)}, u32[]{:S(2)}) collective-permute-start(bf16[26,128,128]{2,1,0:T(8,128)(2,1)} %get-tuple-element.79), channel_id=1, source_target_pairs={{0,2},{1,3},{2,0},{3,1},{4,6},{5,7},{6,4},{7,5},{8,10},{9,11},{10,... | collective-permute-start | bytes 2555912 | tf_op jit(solution)/shard_map/ppermute | solution.py:640
  48.9 39.1 %collective-permute-start.3 = (bf16[26,128,128]{2,1,0:T(8,128)(2,1)}, bf16[26,128,128]{2,1,0:T(8,128)(2,1)}, u32[]{:S(2)}, u32[]{:S(2)}) collective-permute-start(bf16[26,128,128]{2,1,0:T(8,128)(2,1)} %get-tuple-element.80), channel_id=1, source_target_pairs={{0,3},{1,2},{2,1},{3,0},{4,7},{5,6},{6,5},{7,4},{8,11},{9,10},{10,... | collective-permute-start | bytes 2555912 | tf_op jit(solution)/shard_map/ppermute | solution.py:640
  50.0 1.0 copy-start.3
  53.6 53.4 %collective-permute-start.5 = (bf16[2,13,128,128]{3,2,1,0:T(8,128)(2,1)}, bf16[2,13,128,128]{3,2,1,0:T(8,128)(2,1)S(1)}, u32[]{:S(2)}, u32[]{:S(2)}) collective-permute-start(bf16[2,13,128,128]{3,2,1,0:T(8,128)(2,1)} %get-tuple-element.99), channel_id=1, source_target_pairs={{0,4},{4,8},{8,12},{12,16},{16,20},{20,24},{24,28},{28,32},{32,36}... | collective-permute-start | bytes 2555912 | tf_op jit(solution)/shard_map/ppermute | solution.py:658
  55.5 51.5 %collective-permute-start.6 = (bf16[2,13,128,128]{3,2,1,0:T(8,128)(2,1)}, bf16[2,13,128,128]{3,2,1,0:T(8,128)(2,1)}, u32[]{:S(2)}, u32[]{:S(2)}) collective-permute-start(bf16[2,13,128,128]{3,2,1,0:T(8,128)(2,1)} %get-tuple-element.100), channel_id=1, source_target_pairs={{4,0},{8,4},{12,8},{16,12},{20,16},{24,20},{28,24},{32,28},{36,32}... | collective-permute-start | bytes 2555912 | tf_op jit(solution)/shard_map/ppermute | solution.py:659
  90.6 16.4 %copy-start.19 = (bf16[9,128,128]{2,1,0:T(8,128)(2,1)S(1)}, bf16[9,128,128]{2,1,0:T(8,128)(2,1)}, u32[]{:S(2)}) copy-start(bf16[9,128,128]{2,1,0:T(8,128)(2,1)} %get-tuple-element.117) | copy-start | bytes 884740
  90.6 17.4 %copy-start.18 = (bf16[9,128,128]{2,1,0:T(8,128)(2,1)S(1)}, bf16[9,128,128]{2,1,0:T(8,128)(2,1)}, u32[]{:S(2)}) copy-start(bf16[9,128,128]{2,1,0:T(8,128)(2,1)} %get-tuple-element.122) | copy-start | bytes 884740
  90.6 17.4 %copy-start.17 = (bf16[9,128,128]{2,1,0:T(8,128)(2,1)S(1)}, bf16[9,128,128]{2,1,0:T(8,128)(2,1)}, u32[]{:S(2)}) copy-start(bf16[9,128,128]{2,1,0:T(8,128)(2,1)} %get-tuple-element.123) | copy-start | bytes 884740
  90.6 22.7 %copy-start.16 = (bf16[2,13,128,128]{3,2,1,0:T(8,128)(2,1)S(1)}, bf16[2,13,128,128]{3,2,1,0:T(8,128)(2,1)}, u32[]{:S(2)}) copy-start(bf16[2,13,128,128]{3,2,1,0:T(8,128)(2,1)} %get-tuple-element.119) | copy-start | bytes 2555908
  107.0 37.3 %copy-start.9 = (bf16[2,13,128,128]{3,2,1,0:T(8,128)(2,1)}, bf16[2,13,128,128]{3,2,1,0:T(8,128)(2,1)S(1)}, u32[]{:S(2)}) copy-start(bf16[2,13,128,128]{3,2,1,0:T(8,128)(2,1)S(1)} %collective-permute-done.5.refs_2_) | copy-start | bytes 2555908
  107.0 4.4 %collective-permute-start.7 = (bf16[9,128,128]{2,1,0:T(8,128)(2,1)S(1)}, bf16[9,128,128]{2,1,0:T(8,128)(2,1)S(1)}, u32[]{:S(2)}, u32[]{:S(2)}) collective-permute-start(bf16[9,128,128]{2,1,0:T(8,128)(2,1)S(1)} %copy-done.19), channel_id=1, source_target_pairs={{0,1},{1,0},{2,3},{3,2},{4,5},{5,4},{6,7},{7,6},{8,9},{9,8},{10,11... | collective-permute-start | bytes 884744 | tf_op jit(solution)/shard_map/ppermute | solution.py:640
  108.0 12.9 %collective-permute-start.10 = (bf16[9,128,128]{2,1,0:T(8,128)(2,1)S(1)}, bf16[9,128,128]{2,1,0:T(8,128)(2,1)S(1)}, u32[]{:S(2)}, u32[]{:S(2)}) collective-permute-start(bf16[9,128,128]{2,1,0:T(8,128)(2,1)S(1)} %copy-done.18), channel_id=1, source_target_pairs={{0,2},{1,3},{2,0},{3,1},{4,6},{5,7},{6,4},{7,5},{8,10},{9,11},{10,... | collective-permute-start | bytes 884744 | tf_op jit(solution)/shard_map/ppermute | solution.py:640
  108.0 17.2 %collective-permute-start.11 = (bf16[9,128,128]{2,1,0:T(8,128)(2,1)S(1)}, bf16[9,128,128]{2,1,0:T(8,128)(2,1)S(1)}, u32[]{:S(2)}, u32[]{:S(2)}) collective-permute-start(bf16[9,128,128]{2,1,0:T(8,128)(2,1)S(1)} %copy-done.17), channel_id=1, source_target_pairs={{0,3},{1,2},{2,1},{3,0},{4,7},{5,6},{6,5},{7,4},{8,11},{9,10},{10,... | collective-permute-start | bytes 884744 | tf_op jit(solution)/shard_map/ppermute | solution.py:640
  111.4 13.8 %copy-start.6 = (bf16[9,128,128]{2,1,0:T(8,128)(2,1)}, bf16[9,128,128]{2,1,0:T(8,128)(2,1)S(1)}, u32[]{:S(2)}) copy-start(bf16[9,128,128]{2,1,0:T(8,128)(2,1)S(1)} %collective-permute-done.7.refs_7_.refs_1_) | copy-start | bytes 884740
  111.4 32.9 %collective-permute-start.8 = (bf16[2,13,128,128]{3,2,1,0:T(8,128)(2,1)}, bf16[2,13,128,128]{3,2,1,0:T(8,128)(2,1)}, u32[]{:S(2)}, u32[]{:S(2)}) collective-permute-start(bf16[2,13,128,128]{3,2,1,0:T(8,128)(2,1)} %get-tuple-element.118), channel_id=1, source_target_pairs={{0,4},{4,8},{8,12},{12,16},{16,20},{20,24},{24,28},{28,32},{32,36}... | collective-permute-start | bytes 2555912 | tf_op jit(solution)/shard_map/ppermute | solution.py:680
  113.3 31.0 %collective-permute-start.9 = (bf16[2,13,128,128]{3,2,1,0:T(8,128)(2,1)S(1)}, bf16[2,13,128,128]{3,2,1,0:T(8,128)(2,1)}, u32[]{:S(2)}, u32[]{:S(2)}) collective-permute-start(bf16[2,13,128,128]{3,2,1,0:T(8,128)(2,1)S(1)} %copy-done.16), channel_id=1, source_target_pairs={{4,0},{8,4},{12,8},{16,12},{20,16},{24,20},{28,24},{32,28},{36,32}... | collective-permute-start | bytes 2555912 | tf_op jit(solution)/shard_map/ppermute | solution.py:681
  120.9 4.3 %copy-start.7 = (bf16[9,128,128]{2,1,0:T(8,128)(2,1)}, bf16[9,128,128]{2,1,0:T(8,128)(2,1)S(1)}, u32[]{:S(2)}) copy-start(bf16[9,128,128]{2,1,0:T(8,128)(2,1)S(1)} %collective-permute-done.10.refs_8_.refs_2_) | copy-start | bytes 884740
  125.2 0.7 copy-start.8
  128.5 29.8 %collective-permute-start.12 = (bf16[4,5,128,128]{3,2,1,0:T(8,128)(2,1)}, bf16[4,5,128,128]{3,2,1,0:T(8,128)(2,1)S(1)}, u32[]{:S(2)}, u32[]{:S(2)}) collective-permute-start(bf16[4,5,128,128]{3,2,1,0:T(8,128)(2,1)} %get-tuple-element.125), channel_id=1, source_target_pairs={{0,4},{4,8},{8,12},{12,16},{16,20},{20,24},{24,28},{28,32},{32,36}... | collective-permute-start | bytes 1966088 | tf_op jit(solution)/shard_map/ppermute | solution.py:683
  130.4 27.9 %collective-permute-start.13 = (bf16[4,5,128,128]{3,2,1,0:T(8,128)(2,1)}, bf16[4,5,128,128]{3,2,1,0:T(8,128)(2,1)S(1)}, u32[]{:S(2)}, u32[]{:S(2)}) collective-permute-start(bf16[4,5,128,128]{3,2,1,0:T(8,128)(2,1)} %get-tuple-element.126), channel_id=1, source_target_pairs={{4,0},{8,4},{12,8},{16,12},{20,16},{24,20},{28,24},{32,28},{36,32}... | collective-permute-start | bytes 1966088 | tf_op jit(solution)/shard_map/ppermute | solution.py:684
  158.2 0.8 copy-start.4
  158.2 1.1 copy-start.5
  164.8 11.3 %collective-permute-start.17 = (bf16[272,512]{1,0:T(8,128)(2,1)}, bf16[272,512]{1,0:T(8,128)(2,1)S(1)}, u32[]{:S(2)}, u32[]{:S(2)}) collective-permute-start(bf16[272,512]{1,0:T(8,128)(2,1)} %get-tuple-element.133), channel_id=1, source_target_pairs={{0,1},{1,0},{2,3},{3,2},{4,5},{5,4},{6,7},{7,6},{8,9},{9,8},{10,11... | collective-permute-start | bytes 835592 | tf_op jit(solution)/shard_map/ppermute | solution.py:640
  166.2 12.5 %collective-permute-start.18 = (bf16[272,512]{1,0:T(8,128)(2,1)}, bf16[272,512]{1,0:T(8,128)(2,1)S(1)}, u32[]{:S(2)}, u32[]{:S(2)}) collective-permute-start(bf16[272,512]{1,0:T(8,128)(2,1)} %get-tuple-element.134), channel_id=1, source_target_pairs={{0,2},{1,3},{2,0},{3,1},{4,6},{5,7},{6,4},{7,5},{8,10},{9,11},{10,... | collective-permute-start | bytes 835592 | tf_op jit(solution)/shard_map/ppermute | solution.py:640
  167.2 15.6 %collective-permute-start.19 = (bf16[272,512]{1,0:T(8,128)(2,1)}, bf16[272,512]{1,0:T(8,128)(2,1)S(1)}, u32[]{:S(2)}, u32[]{:S(2)}) collective-permute-start(bf16[272,512]{1,0:T(8,128)(2,1)} %get-tuple-element.135), channel_id=1, source_target_pairs={{0,3},{1,2},{2,1},{3,0},{4,7},{5,6},{6,5},{7,4},{8,11},{9,10},{10,... | collective-permute-start | bytes 835592 | tf_op jit(solution)/shard_map/ppermute | solution.py:640
  175.0 12.4 %collective-permute-start.16 = (bf16[272,512]{1,0:T(8,128)(2,1)}, bf16[272,512]{1,0:T(8,128)(2,1)S(1)}, u32[]{:S(2)}, u32[]{:S(2)}) collective-permute-start(bf16[272,512]{1,0:T(8,128)(2,1)} %get-tuple-element.130), channel_id=1, source_target_pairs={{0,1},{1,0},{2,3},{3,2},{4,5},{5,4},{6,7},{7,6},{8,9},{9,8},{10,11... | collective-permute-start | bytes 835592 | tf_op jit(solution)/shard_map/ppermute | solution.py:640
  175.2 15.8 %collective-permute-start.15 = (bf16[272,512]{1,0:T(8,128)(2,1)}, bf16[272,512]{1,0:T(8,128)(2,1)S(1)}, u32[]{:S(2)}, u32[]{:S(2)}) collective-permute-start(bf16[272,512]{1,0:T(8,128)(2,1)} %get-tuple-element.128), channel_id=1, source_target_pairs={{0,2},{1,3},{2,0},{3,1},{4,6},{5,7},{6,4},{7,5},{8,10},{9,11},{10,... | collective-permute-start | bytes 835592 | tf_op jit(solution)/shard_map/ppermute | solution.py:640
  176.1 6.7 %copy-start.11 = (bf16[272,512]{1,0:T(8,128)(2,1)}, bf16[272,512]{1,0:T(8,128)(2,1)S(1)}, u32[]{:S(2)}) copy-start(bf16[272,512]{1,0:T(8,128)(2,1)S(1)} %collective-permute-done.17.refs_1_) | copy-start | bytes 835588
  176.1 18.1 %collective-permute-start.14 = (bf16[272,512]{1,0:T(8,128)(2,1)}, bf16[272,512]{1,0:T(8,128)(2,1)S(1)}, u32[]{:S(2)}, u32[]{:S(2)}) collective-permute-start(bf16[272,512]{1,0:T(8,128)(2,1)} %get-tuple-element.127), channel_id=1, source_target_pairs={{0,3},{1,2},{2,1},{3,0},{4,7},{5,6},{6,5},{7,4},{8,11},{9,10},{10,... | collective-permute-start | bytes 835592 | tf_op jit(solution)/shard_map/ppermute | solution.py:640
  178.7 4.1 %copy-start.12 = (bf16[272,512]{1,0:T(8,128)(2,1)}, bf16[272,512]{1,0:T(8,128)(2,1)S(1)}, u32[]{:S(2)}) copy-start(bf16[272,512]{1,0:T(8,128)(2,1)S(1)} %collective-permute-done.18.refs_2_) | copy-start | bytes 835588
  182.8 0.7 copy-start.14
  187.4 0.7 copy-start.15
  191.0 0.7 copy-start.13
  194.2 0.7 copy-start.10
